TPU v7x, 32 devices: a whole 2x2x4 slice. The times are simulated.
32 devices in a mesh: snap: 2 (over y), curve: 4 (over z), chan: 2 (over x), rep: 2 (over core).
Axes of the slice: x: 2, y: 2, z: 4, core: 2. Of those that a mesh axis runs over, the one named last changes fastest.
Arguments:
- children: bfloat16 [8, 128, 12288], P(None, None, ('snap', 'curve', 'rep')), parts along dimension 2, may hold values from -6 to 6
- child_mask: int32 [8, 12288], P(None, ('snap', 'curve', 'rep')), parts along dimension 1, may hold values from 0 to 1, as said below
- neighbours: int32 [27, 12288], P(None, ('snap', 'curve', 'rep')), parts along dimension 1, may hold values from -1 to 6143, as said below
- down_weight: bfloat16 [8, 256, 128], P(None, 'chan'), may hold values from -0.25 to 0.25
- conv_weight: bfloat16 [27, 256, 256], P(None, 'chan'), may hold values from -0.125 to 0.125
- cotangent: bfloat16 [256, 12288], P('chan', ('snap', 'curve', 'rep')), parts along dimension 1, may hold values from -6 to 6
Outputs:
- features_out: bfloat16 [256, 12288], P('chan', ('snap', 'curve', 'rep')), parts along dimension 1
- children_grad: bfloat16 [8, 128, 12288], P(None, 'chan', ('snap', 'curve', 'rep')), parts along dimension 2
- conv_weight_grad: float32 [54, 256, 256], P('snap', 'chan'), parts along dimension 0
- down_weight_grad: float32 [16, 256, 128], P('snap', 'chan'), parts along dimension 0
There are 2 independent parts, one for each index of `snap`. A program takes and returns all parts, laid end to end along the dimension named above; an argument that names none is the same for every part. Nothing has to cross between parts.
Inputs may be any that keep to these rules, and one draw needn't show every extreme that they name: Entry k of site p names the slot of the site at offset (k // 9 - 1, k // 3 % 3 - 1, k % 3 - 1) cells from p, or -1 where that cell is empty; entry 13 of an occupied site is p itself; neighbours[26 - k, neighbours[k, p]] = p wherever neighbours[k, p] >= 0; a site in slots j * 768 to (j + 1) * 768 - 1 names only sites in slots (j - 1) * 768 to (j + 2) * 768 - 1; empty slots hold -1 in all 27 entries. `child_mask`: 1 where the child cell is occupied; every occupied coarse site has at least one occupied child, empty slots have none.
All inputs are finite; a program needn't handle non-finite values.
Results may differ from a plain program's by a relative error of at most 0.0067.
Values may be sent and summed in bfloat16 or wider, within the bound.
No kernel may reach another device: no remote copies, remote signals or barrier semaphores. Data moves between devices by JAX's collectives and lax.ppermute only.
A program may use at most 128 MiB of HBM per device.

v0:
```python
import functools

import jax
import jax.numpy as jnp
from jax import lax
from jax.experimental import pallas as pl
from jax.experimental.pallas import tpu as pltpu
from jax.sharding import PartitionSpec as P

BLOCK = 128
SPAN = 256
GROUPS = 3
PER = 9
VMEM_LIMIT = 28 * 1024 * 1024
WHOLE_LIMIT = 60 * 1024 * 1024
PIECES = ("curve", "rep")
F32 = jnp.float32
BF16 = jnp.bfloat16
NOWHERE = -(2**20)
NT = (((1,), (1,)), ((), ()))


def silu_slope(value):
    sigma = jax.nn.sigmoid(value)
    return sigma * (1.0 + value * (1.0 - sigma))


def met(shard):
    devices = lax.axis_size(PIECES)
    pairs = [(i, i + 1) for i in range(1, devices - 1, 2)]
    pairs += [(j, i) for i, j in pairs]
    return [lax.ppermute(shard, PIECES, pairs), swapped(shard, "rep")]


def swapped(shard, axis):
    return lax.ppermute(shard, axis, [(0, 1), (1, 0)])


def call(kernel, out_shape, in_specs, scratch, out_specs=None, limit=VMEM_LIMIT):
    options = {} if out_specs is None else {"out_specs": out_specs}
    return pl.pallas_call(
        kernel,
        out_shape=out_shape,
        in_specs=in_specs,
        scratch_shapes=scratch,
        compiler_params=pltpu.CompilerParams(vmem_limit_bytes=limit),
        cost_estimate=pl.CostEstimate(flops=0, bytes_accessed=0, transcendentals=0),
        **options,
    )


def anywhere(count):
    return [pl.BlockSpec(memory_space=pl.ANY)] * count


def vmem(count):
    return [pl.BlockSpec(memory_space=pltpu.VMEM)] * count


SMEM = [pl.BlockSpec(memory_space=pltpu.SMEM)]


def down_kernel(children_ref, mask_ref, weight_ref, coarse_ref, slope_ref):
    octants = children_ref.shape[0]
    total = None
    for o in range(0, octants, 2):
        masked = jnp.concatenate(
            [
                children_ref[o + j] * mask_ref[o + j : o + j + 1, :].astype(F32).astype(BF16)
                for j in range(2)
            ],
            axis=0,
        )
        weights = jnp.concatenate([weight_ref[o], weight_ref[o + 1]], axis=1)
        term = jnp.dot(weights, masked, preferred_element_type=F32)
        total = term if total is None else total + term
    slope_ref[...] = silu_slope(total)
    coarse_ref[...] = (total * jax.nn.sigmoid(total)).T.astype(BF16)


def index_kernel(shards, neighbours_ref, index_ref, scalars_ref):
    offsets, rows = neighbours_ref.shape
    blocks = rows // BLOCK
    curve, rep = lax.axis_index("curve"), lax.axis_index("rep")
    names = neighbours_ref[...]
    local = jnp.where(names >= 0, names - (curve * 2 + rep - 1) * rows, NOWHERE)
    index_ref[...] = jnp.full(index_ref.shape, NOWHERE, jnp.int32)
    for group in range(GROUPS):
        part = local[group * PER : (group + 1) * PER]
        index_ref[group, :PER, :] = part
        lows = jnp.min(jnp.where(part < 0, -NOWHERE, part), axis=0, keepdims=True)
        highs = jnp.max(part, axis=0, keepdims=True)
        for block in range(blocks):
            at = slice(block * BLOCK, (block + 1) * BLOCK)
            low, high = jnp.min(lows[:, at]), jnp.max(highs[:, at]) + 1
            low = jnp.where(high <= 0, 0, low // 16 * 16)
            steps = jnp.maximum(1, (high - low + SPAN - 1) // SPAN)
            scalars_ref[group * blocks + block] = low
            scalars_ref[(GROUPS + group) * blocks + block] = steps
    last = 2 * GROUPS * blocks
    scalars_ref[last] = lax.axis_index("chan")
    scalars_ref[last + 1] = curve if shards > 1 else 0
    scalars_ref[last + 2] = rep


def fill_window(window_ref, parts, slots, rep):
    rows = parts[0][0].shape[0]
    places = (rows, rep * 2 * rows, (1 - rep) * 2 * rows)
    for part, slot in zip(parts, slots):
        for source, place in zip(part, places):
            window_ref[slot, pl.ds(pl.multiple_of(place, 16), rows), :] = source[...]
    blank = (window_ref.shape[0], window_ref.shape[1] - 3 * rows, window_ref.shape[2])
    window_ref[:, 3 * rows :, :] = jnp.zeros(blank, BF16)


def gather(scalars_ref, column_ref, window_ref, blocks, store, add):
    lanes = lax.broadcasted_iota(jnp.int32, (BLOCK, SPAN), 1).astype(F32).astype(BF16)

    def picked(group, rows, start):
        columns = jnp.clip(column_ref[group, rows, :] - start, -1, SPAN).astype(F32).astype(BF16)
        hot = [
            jnp.where(
                jnp.broadcast_to(columns[:, j : j + 1], (BLOCK, SPAN)) == lanes,
                jnp.ones((), BF16),
                jnp.zeros((), BF16),
            )
            for j in range(PER)
        ]
        at = pl.ds(pl.multiple_of(start, 16), SPAN)
        span = jnp.concatenate([window_ref[c, at, :] for c in range(window_ref.shape[0])], axis=1)
        return jnp.dot(jnp.concatenate(hot, axis=0), span, preferred_element_type=F32).astype(BF16)

    def first(block, _):
        rows = pl.ds(pl.multiple_of(block * BLOCK, BLOCK), BLOCK)
        for group in range(GROUPS):
            result = picked(group, rows, scalars_ref[group * blocks + block])
            for j in range(PER):
                store(group, j, rows, result[j * BLOCK : (j + 1) * BLOCK])
        return 0

    lax.fori_loop(0, blocks, first, 0, unroll=3)

    def rest(at, _):
        group, block = at // blocks, at % blocks
        rows = pl.ds(pl.multiple_of(block * BLOCK, BLOCK), BLOCK)

        def more(step, _):
            result = picked(group, rows, scalars_ref[at] + step * SPAN)
            for j in range(PER):
                add(group, j, rows, result[j * BLOCK : (j + 1) * BLOCK])
            return 0

        lax.fori_loop(1, scalars_ref[GROUPS * blocks + at], more, 0)
        return 0

    lax.fori_loop(0, GROUPS * blocks, rest, 0)


def turn(scratch_ref, value, shards, scalars_ref, at):
    half = value.shape[0] // 2
    size = half // shards
    scratch_ref[0] = value
    place = 0 if shards == 1 else scalars_ref[at + 1]
    rep = scalars_ref[at + 2]
    for core in range(2):
        for step in range(shards):
            source = (rep + core) % 2 * half + (place ^ step) * size
            target = core * half + step * size
            scratch_ref[1, target : target + size] = scratch_ref[
                0, pl.ds(pl.multiple_of(source, size), size)
            ]


def conv_kernel(chans, shards, scale, scalars_ref, index_ref, weight_ref, cotangent_ref, *refs):
    parts, refs = [refs[3 * i : 3 * i + 3] for i in range(chans)], refs[3 * chans :]
    out_ref, grad_ref, keep_ref, send_ref = refs[:4]
    window_ref, column_ref, picked_ref, conv_ref, scratch_ref = refs[4:]
    rows = index_ref.shape[2]
    blocks = rows // BLOCK
    width = chans * window_ref.shape[2]
    channels = weight_ref.shape[1]
    chan = scalars_ref[2 * GROUPS * blocks]
    rep = scalars_ref[2 * GROUPS * blocks + 2]
    slots = (chan, 1 - chan) if chans == 2 else range(chans)
    fill_window(window_ref, parts, slots, rep)
    for group in range(GROUPS):
        column_ref[group] = index_ref[group].T

    def store(group, j, at, value):
        lane = j % 3 * width
        picked_ref[group * 3 + j // 3, at, lane : lane + width] = value

    def add(group, j, at, value):
        lane = j % 3 * width
        picked_ref[group * 3 + j // 3, at, lane : lane + width] += value

    gather(scalars_ref, column_ref, window_ref, blocks, store, add)

    def multiply(three, _):
        weights = jnp.concatenate([weight_ref[three * 3 + j] for j in range(3)], axis=1)
        term = lax.dot_general(picked_ref[three], weights, NT, preferred_element_type=F32)
        conv_ref[...] += term
        return 0

    conv_ref[...] = jnp.zeros_like(conv_ref)
    lax.fori_loop(0, 9, multiply, 0, unroll=3)
    conv = conv_ref[...].T
    sigma = jax.nn.sigmoid(conv)
    out_ref[...] = (conv * sigma).astype(BF16)
    grad = cotangent_ref[...].astype(F32) * (sigma * (1.0 + conv * (1.0 - sigma)))
    grad_ref[...] = grad.T.astype(BF16)
    turn(scratch_ref, grad.astype(BF16), shards, scalars_ref, 2 * GROUPS * blocks)
    half = channels // 2
    size = half // shards

    def weigh(three, _):
        term = jnp.dot(scratch_ref[1], picked_ref[three], preferred_element_type=F32) * scale
        for j in range(3):
            both = term[:, j * width : (j + 1) * width].astype(BF16)
            for step in range(shards):
                at = step * size
                keep_ref[step, three * 3 + j] = both[at : at + size]
                send_ref[step, three * 3 + j] = both[half + at : half + at + size]
        return 0

    lax.fori_loop(0, 9, weigh, 0, unroll=3)


def coarse_grad_kernel(scalars_ref, index_ref, weight_ref, *refs):
    part, refs = refs[:3], refs[3:]
    mine_ref, other_ref, window_ref, column_ref, picked_ref, total_ref = refs
    rows = index_ref.shape[2]
    blocks = rows // BLOCK
    offsets, channels, width = weight_ref.shape
    chan = scalars_ref[2 * GROUPS * blocks]
    rep = scalars_ref[2 * GROUPS * blocks + 2]
    fill_window(window_ref, [part], (0,), rep)
    for group in range(GROUPS):
        column_ref[group] = index_ref[group].T

    def store(group, j, at, value):
        lane = (PER - 1 - j) * channels
        picked_ref[GROUPS - 1 - group, at, lane : lane + channels] = value

    def add(group, j, at, value):
        lane = (PER - 1 - j) * channels
        picked_ref[GROUPS - 1 - group, at, lane : lane + channels] += value

    gather(scalars_ref, column_ref, window_ref, blocks, store, add)
    result = None
    for group in range(GROUPS):
        weights = weight_ref[group * PER : (group + 1) * PER].reshape(PER * channels, width)
        term = jnp.dot(picked_ref[group], weights, preferred_element_type=F32)
        result = term if result is None else result + term
    result = result.T
    chans = width // channels
    for at in range(chans):
        total_ref[at] = result[at * channels : (at + 1) * channels]
    mine_ref[...] = total_ref[chan]
    for step in range(1, chans):
        other_ref[step - 1] = total_ref[lax.rem(chan + step, chans)].astype(BF16)


def pre_grad_kernel(scale, scalars_ref, children_ref, mask_ref, slope_ref, mine_ref, *refs):
    others, (grad_ref, keep_ref, send_ref, scratch_ref) = refs[:-4], refs[-4:]
    total = mine_ref[...]
    for other in others:
        total = total + other[...].astype(F32)
    grad = (total * slope_ref[...]).astype(BF16)
    grad_ref[...] = grad
    blocks = grad.shape[1] // BLOCK
    turn(scratch_ref, grad, 1, scalars_ref, 2 * GROUPS * blocks)
    half = grad.shape[0] // 2
    fine = children_ref.shape[1]
    for o in range(0, children_ref.shape[0], 2):
        masked = jnp.concatenate(
            [
                children_ref[o + j] * mask_ref[o + j : o + j + 1, :].astype(F32).astype(BF16)
                for j in range(2)
            ],
            axis=0,
        )
        term = lax.dot_general(scratch_ref[1], masked, NT, preferred_element_type=F32) * scale
        both = term.astype(BF16)
        for j in range(2):
            keep_ref[o + j] = both[:half, j * fine : (j + 1) * fine]
            send_ref[o + j] = both[half:, j * fine : (j + 1) * fine]


def cut_kernel(weight_ref, *refs):
    out_refs, scratch_ref = refs[:-1], refs[-1]
    octants, fine, _ = scratch_ref.shape
    chans = len(out_refs)
    size = fine // chans
    chan = lax.axis_index("chan")
    for o in range(octants):
        scratch_ref[o] = weight_ref[o].T
    for by in range(chans):
        at = pl.ds(pl.multiple_of((chan + by) % chans * size, size), size)
        for o in range(octants):
            out_refs[by][o] = scratch_ref[o, at, :]


def children_kernel(mask_ref, *refs):
    out_hbm, out_ref, sems = refs[-3:]
    count = (len(refs) - 3) // 2
    grads, weights = refs[:count], refs[count:-3]
    copies = []
    for o in range(out_ref.shape[0]):
        total = None
        for grad, weight in zip(grads, weights):
            term = jnp.dot(weight[o], grad[...], preferred_element_type=F32)
            term = term.astype(BF16).astype(F32)
            total = term if total is None else total + term
        out_ref[o] = (total * mask_ref[o : o + 1, :].astype(F32)).astype(BF16)
        copies.append(pltpu.make_async_copy(out_ref.at[o], out_hbm.at[o], sems.at[o]))
        copies[-1].start()
    for copy in copies:
        copy.wait()


def apart(shard, by):
    return lax.ppermute(shard, "curve", [(i, i ^ by) for i in range(lax.axis_size("curve"))])


def added(*terms):
    return sum(term.astype(F32) for term in terms).astype(BF16)


def sum_over_curve(total, beside):
    terms = [apart(total[by], by) for by in range(1, 4)]
    own = added(after(total[0], beside), *terms)
    across = apart(own, 2)
    return [own, apart(own, 1), across, apart(across, 1)]


def after(value, *earlier):
    return lax.optimization_barrier((value, *earlier))[0]


def body(children, child_mask, neighbours, down_weight, conv_weight, cotangent):
    octants, fine, rows = children.shape
    offsets, channels, width = conv_weight.shape
    blocks = rows // BLOCK
    chans = lax.axis_size("chan")
    chan = lax.axis_index("chan")
    rep = lax.axis_index("rep")
    curve = lax.axis_index("curve")
    pieces = lax.axis_size(PIECES)
    scale = 1.0 / (rows * pieces) ** 0.5
    shape = jax.ShapeDtypeStruct
    half = channels // 2
    shards = 4 if lax.axis_size("curve") == 4 and half % 64 == 0 else 1
    size = half // shards

    coarse, slope = call(
        down_kernel,
        [shape((rows, channels), BF16), shape((channels, rows), F32)],
        vmem(3),
        [],
        limit=WHOLE_LIMIT,
    )(children, child_mask, down_weight)

    if chans == 2:
        parts = [coarse, swapped(coarse, "chan")]
    else:
        every = lax.all_gather(coarse, "chan", axis=0)
        parts = [every[i] for i in range(chans)]
    windows = [array for part in parts for array in [part] + met(part)]
    conv_weight = conv_weight * after(jnp.ones((), BF16), coarse)
    index, scalars = call(
        functools.partial(index_kernel, shards),
        [shape((GROUPS, 16, rows), jnp.int32), shape((2 * GROUPS * blocks + 3,), jnp.int32)],
        vmem(1),
        [],
        vmem(1) + SMEM,
    )(after(neighbours, parts[1]))

    features_out, conv_grad, keep, send = call(
        functools.partial(conv_kernel, chans, shards, scale),
        [
            shape((channels, rows), BF16),
            shape((rows, channels), BF16),
            shape((shards, offsets, size, width), BF16),
            shape((shards, offsets, size, width), BF16),
        ],
        SMEM + vmem(3 + 3 * chans),
        [
            pltpu.VMEM((chans, 3 * rows + SPAN, channels), BF16),
            pltpu.VMEM((GROUPS, rows, 16), jnp.int32),
            pltpu.VMEM((9, rows, 3 * width), BF16),
            pltpu.VMEM((rows, channels), F32),
            pltpu.VMEM((2, channels, rows), BF16),
        ],
    )(scalars, index, conv_weight, cotangent, *windows)

    near = met(conv_grad)
    received = swapped(send, "rep")
    total = [added(keep[i], received[i]) for i in range(shards)]

    mine, others = call(
        coarse_grad_kernel,
        [shape((channels, rows), F32), shape((chans - 1, channels, rows), BF16)],
        SMEM + vmem(5),
        [
            pltpu.VMEM((1, 3 * rows + SPAN, channels), BF16),
            pltpu.VMEM((GROUPS, rows, 16), jnp.int32),
            pltpu.VMEM((GROUPS, rows, PER * channels), BF16),
            pltpu.VMEM((chans, channels, rows), F32),
        ],
    )(after(scalars, *total), index, conv_weight, conv_grad, *near)
    received = [
        lax.ppermute(others[by - 1], "chan", [(i, (i + by) % chans) for i in range(chans)])
        for by in range(1, chans)
    ]
    mine_fine = fine // chans
    cut = call(
        cut_kernel,
        [shape((octants, mine_fine, channels), BF16)] * chans,
        vmem(1),
        [pltpu.VMEM((octants, fine, channels), BF16)],
    )(after(down_weight, mine))
    blank = [
        jnp.broadcast_to(after(jnp.zeros((), F32), mine), like.shape)
        for like in (conv_weight, down_weight)
    ]
    pre_grad, keep, send = call(
        functools.partial(pre_grad_kernel, scale),
        [
            shape((channels, rows), BF16),
            shape((octants, half, fine), BF16),
            shape((octants, half, fine), BF16),
        ],
        SMEM + vmem(4 + len(received)),
        [pltpu.VMEM((2, channels, rows), BF16)],
    )(after(scalars, *cut, *blank), children, child_mask, slope, mine, *received)

    if shards == 4:
        sums = sum_over_curve(total, pre_grad)
    else:
        sums = [lax.psum(total[0], "curve")]
    own = sums[0]
    sent_grad, send = after(pre_grad, own), after(send, own)
    grads = [
        lax.ppermute(sent_grad, "chan", [(i, (i + by) % chans) for i in range(chans)])
        if by
        else pre_grad
        for by in range(chans)
    ]
    weights = [
        lax.ppermute(after(cut[by], own), "chan", [(i, (i + by) % chans) for i in range(chans)])
        if by
        else cut[by]
        for by in range(chans)
    ]
    children_grad = call(
        children_kernel,
        shape((octants, mine_fine, rows), BF16),
        vmem(1 + 2 * chans),
        [pltpu.VMEM((octants, mine_fine, rows), BF16), pltpu.SemaphoreType.DMA((octants,))],
        anywhere(1)[0],
    )(after(child_mask, *sums[2:3]), *grads, *weights)

    down = added(keep, swapped(send, "rep"))
    if shards == 4:
        down = added(down, apart(down, 1))
        down = added(after(down, children_grad), apart(down, 2))
    else:
        down = lax.psum(down, "curve")
    def joined(result, pieces):
        for row, piece in pieces:
            result = lax.dynamic_update_slice(result, piece.astype(F32), (0, row, 0))
        return result

    rows_of = [rep * half, (1 - rep) * half]
    down_weight_grad = joined(blank[1], zip(rows_of, (down, swapped(down, "rep"))))
    pieces = []
    for step, part in enumerate(sums):
        at = (curve ^ step) * size if shards > 1 else 0
        mine = part if step else after(part, *sums[2:3])
        pieces += [(rows_of[0] + at, mine), (rows_of[1] + at, swapped(part, "rep"))]
    conv_weight_grad = joined(blank[0], pieces)
    return (features_out, children_grad, conv_weight_grad, down_weight_grad)


def solution(mesh):
    in_specs = (
        P(None, None, ("snap", "curve", "rep")),
        P(None, ("snap", "curve", "rep")),
        P(None, ("snap", "curve", "rep")),
        P(None, "chan", None),
        P(None, "chan", None),
        P("chan", ("snap", "curve", "rep")),
    )
    out_specs = (
        P("chan", ("snap", "curve", "rep")),
        P(None, "chan", ("snap", "curve", "rep")),
        P("snap", "chan", None),
        P("snap", "chan", None),
    )
    return jax.shard_map(body, mesh=mesh, in_specs=in_specs, out_specs=out_specs, check_vma=False)
```

profile of v0, /device:TPU:0, one launch (start us, length us, event | category | flops | bytes accessed | tf_op | source)
XLA Modules:
  0.0 87.3 jit_solution(4104481128369511123)
XLA Ops:
  0.7 2.7 %shard_map.93 = (bf16[768,128]{1,0:T(8,128)(2,1)}, f32[128,768]{1,0:T(8,128)}) custom-call(bf16[8,128,768]{2,1,0:T(8,128)(2,1)} %children_ref.3, s32[8,768]{1,0:T(8,128)} %mask_ref.4, bf16[8,128,128]{2,1,0:T(8,128)(2,1)} %weight_ref.2), custom_call_target="tpu_custom_call" | custom-call | tf_op jit(solution)/shard_map/pallas_call | solution.py:356
  3.4 2.9 %collective-permute-start = (bf16[768,128]{1,0:T(8,128)(2,1)}, bf16[768,128]{1,0:T(8,128)(2,1)S(1)}, u32[]{:S(2)}, u32[]{:S(2)}) collective-permute-start(bf16[768,128]{1,0:T(8,128)(2,1)} %get-tuple-element.32.refs_0_), channel_id=1, source_target_pairs={{0,2},{2,0},{1,3},{3,1},{4,6},{6,4},{5,7},{7,5},{8,10},{10,8},{9,1... | collective-permute-start | bytes 589832 | tf_op jit(solution)/shard_map/ppermute | solution.py:36
  6.3 0.7 collective-permute-start.1
  7.0 3.0 %collective-permute-start.2 = (bf16[768,128]{1,0:T(8,128)(2,1)}, bf16[768,128]{1,0:T(8,128)(2,1)S(1)}, u32[]{:S(2)}, u32[]{:S(2)}) collective-permute-start(bf16[768,128]{1,0:T(8,128)(2,1)} %get-tuple-element.32.refs_0_), channel_id=1, source_target_pairs={{0,1},{1,0},{2,3},{3,2},{4,5},{5,4},{6,7},{7,6},{8,9},{9,8},{10,11... | collective-permute-start | bytes 589832 | tf_op jit(solution)/shard_map/ppermute | solution.py:36
  10.0 1.5 %collective-permute-done.refs_3_ = bf16[768,128]{1,0:T(8,128)(2,1)S(1)} collective-permute-done((bf16[768,128]{1,0:T(8,128)(2,1)}, bf16[768,128]{1,0:T(8,128)(2,1)S(1)}, u32[]{:S(2)}, u32[]{:S(2)}) %collective-permute-start) | collective-permute-done | bytes 196640 | tf_op jit(solution)/shard_map/ppermute | solution.py:36
  11.5 0.7 collective-permute-start.3
  12.2 3.2 %collective-permute-start.4 = (bf16[768,128]{1,0:T(8,128)(2,1)S(1)}, bf16[768,128]{1,0:T(8,128)(2,1)S(1)}, u32[]{:S(2)}, u32[]{:S(2)}) collective-permute-start(bf16[768,128]{1,0:T(8,128)(2,1)S(1)} %collective-permute-done.refs_3_), channel_id=1, source_target_pairs={{0,1},{1,0},{2,3},{3,2},{4,5},{5,4},{6,7},{7,6},{8,9},{9,8},{10,11... | collective-permute-start | bytes 589832 | tf_op jit(solution)/shard_map/ppermute | solution.py:36
  15.3 1.6 %broadcast_multiply_fusion.weight_ref = bf16[27,128,256]{2,1,0:T(8,128)(2,1)S(1)} fusion(bf16[27,128,256]{2,1,0:T(8,128)(2,1)} %param.10, bf16[]{:T(256)} %constant.3.clone.1), kind=kLoop, calls=%fused_computation | loop fusion | flops 884736 | bytes 3538946 | tf_op jit(solution)/shard_map/mul | solution.py:370
  17.0 1.0 %shard_map.94 = (s32[3,16,768]{2,1,0:T(8,128)S(1)}, s32[39]{0:T(128)S(1)}) custom-call(s32[27,768]{1,0:T(8,128)S(1)} %copy-done.6), custom_call_target="tpu_custom_call" | custom-call | tf_op jit(solution)/shard_map/pallas_call | solution.py:371
  18.1 10.1 %shard_map.95 = (bf16[128,768]{1,0:T(8,128)(2,1)}, bf16[768,128]{1,0:T(8,128)(2,1)S(1)}, bf16[4,27,16,256]{3,2,1,0:T(8,128)(2,1)S(1)}, bf16[4,27,16,256]{3,2,1,0:T(8,128)(2,1)S(1)}) custom-call(s32[39]{0:T(128)S(1)} %get-tuple-element.47.scalars_ref, s32[3,16,768]{2,1,0:T(8,128)S(1)} %get-tuple-element.35.index_ref, ...), custom_call_target="tpu_custom_call" | custom-call | tf_op jit(solution)/shard_map/pallas_call | solution.py:379
  28.2 0.6 collective-permute-start.5
  28.8 0.8 collective-permute-start.6
  29.7 4.0 %collective-permute-start.7 = (bf16[768,128]{1,0:T(8,128)(2,1)S(1)}, bf16[768,128]{1,0:T(8,128)(2,1)S(1)}, u32[]{:S(2)}, u32[]{:S(2)}) collective-permute-start(bf16[768,128]{1,0:T(8,128)(2,1)S(1)} %get-tuple-element.41.refs_0_), channel_id=1, source_target_pairs={{0,1},{1,0},{2,3},{3,2},{4,5},{5,4},{6,7},{7,6},{8,9},{9,8},{10,11... | collective-permute-start | bytes 589832 | tf_op jit(solution)/shard_map/ppermute | solution.py:36
  33.9 2.6 %collective-permute-start.10 = (bf16[27,16,256]{2,1,0:T(8,128)(2,1)S(1)}, bf16[27,16,256]{2,1,0:T(8,128)(2,1)S(1)}, u32[]{:S(2)}, u32[]{:S(2)}) collective-permute-start(bf16[27,16,256]{2,1,0:T(8,128)(2,1)S(1)} %get-tuple-element.64), channel_id=1, source_target_pairs={{0,8},{4,12},{8,0},{12,4},{1,9},{5,13},{9,1},{13,5},{2,10},{6,14},... | collective-permute-start | bytes 663560 | tf_op jit(solution)/shard_map/ppermute | solution.py:323
  36.5 1.7 %collective-permute-start.11 = (bf16[27,16,256]{2,1,0:T(8,128)(2,1)S(1)}, bf16[27,16,256]{2,1,0:T(8,128)(2,1)S(1)}, u32[]{:S(2)}, u32[]{:S(2)}) collective-permute-start(bf16[27,16,256]{2,1,0:T(8,128)(2,1)S(1)} %get-tuple-element.63), channel_id=1, source_target_pairs={{0,12},{4,8},{8,4},{12,0},{1,13},{5,9},{9,5},{13,1},{2,14},{6,10},... | collective-permute-start | bytes 663560 | tf_op jit(solution)/shard_map/ppermute | solution.py:323
  38.2 6.3 %shard_map.96 = (f32[128,768]{1,0:T(8,128)S(1)}, bf16[1,128,768]{2,1,0:T(8,128)(2,1)S(1)}) custom-call(s32[39]{0:T(128)S(1)} %get-tuple-element.47.scalars_ref, s32[3,16,768]{2,1,0:T(8,128)S(1)} %get-tuple-element.35.index_ref, bf16[27,128,256]{2,1,0:T(8,128)(2,1)S(1)} %broadcast_multiply_fusion.weight_ref, bf16[768,128]{1,0:T(8,128)(2,1)S(1)} %get-tuple-element.41.refs_0_, ...), custom_call_target="tpu_custom_call" | custom-call | tf_op jit(solution)/shard_map/pallas_call | solution.py:401
  44.6 1.6 %collective-permute-start.8 = (bf16[128,768]{1,0:T(8,128)(2,1)S(1)}, bf16[128,768]{1,0:T(8,128)(2,1)S(1)}, u32[]{:S(2)}, u32[]{:S(2)}) collective-permute-start(bf16[128,768]{1,0:T(8,128)(2,1)S(1)} %bitcast.9), channel_id=1, source_target_pairs={{0,2},{2,0},{1,3},{3,1},{4,6},{6,4},{5,7},{7,5},{8,10},{10,8},{9,1... | collective-permute-start | bytes 589832 | tf_op jit(solution)/shard_map/ppermute | solution.py:413
  46.3 4.6 %collective-permute-done.8.refs_0_ = bf16[128,768]{1,0:T(8,128)(2,1)S(1)} collective-permute-done((bf16[128,768]{1,0:T(8,128)(2,1)S(1)}, bf16[128,768]{1,0:T(8,128)(2,1)S(1)}, u32[]{:S(2)}, u32[]{:S(2)}) %collective-permute-start.8) | collective-permute-done | bytes 196640 | tf_op jit(solution)/shard_map/ppermute | solution.py:413
  50.9 1.2 %shard_map.98 = (bf16[128,768]{1,0:T(8,128)(2,1)S(1)}, bf16[8,64,128]{2,1,0:T(8,128)(2,1)S(1)}, bf16[8,64,128]{2,1,0:T(8,128)(2,1)S(1)}) custom-call(s32[39]{0:T(128)S(1)} %get-tuple-element.47.scalars_ref, bf16[8,128,768]{2,1,0:T(8,128)(2,1)S(1)} %copy-done, s32[8,768]{1,0:T(8,128)S(1)} %copy-done.3, f32[128,768]{1,0:T(8,128)S(1)} %copy-done.2, ...), custom_call_target="tpu_custom_call" | custom-call | tf_op jit(solution)/shard_map/pallas_call | solution.py:427
  52.1 1.0 %collective-permute-done.10 = bf16[27,16,256]{2,1,0:T(8,128)(2,1)S(1)} collective-permute-done((bf16[27,16,256]{2,1,0:T(8,128)(2,1)S(1)}, bf16[27,16,256]{2,1,0:T(8,128)(2,1)S(1)}, u32[]{:S(2)}, u32[]{:S(2)}) %collective-permute-start.10) | collective-permute-done | bytes 221216 | tf_op jit(solution)/shard_map/ppermute | solution.py:323
  53.4 5.6 %collective-permute-start.12 = (bf16[27,16,256]{2,1,0:T(8,128)(2,1)S(1)}, bf16[27,16,256]{2,1,0:T(8,128)(2,1)S(1)}, u32[]{:S(2)}, u32[]{:S(2)}) collective-permute-start(bf16[27,16,256]{2,1,0:T(8,128)(2,1)S(1)} %add_convert_fusion), channel_id=1, source_target_pairs={{0,8},{4,12},{8,0},{12,4},{1,9},{5,13},{9,1},{13,5},{2,10},{6,14},... | collective-permute-start | bytes 663560 | tf_op jit(solution)/shard_map/ppermute | solution.py:323
  59.1 1.5 %collective-permute-start.14 = (bf16[8,64,128]{2,1,0:T(8,128)(2,1)S(1)}, bf16[8,64,128]{2,1,0:T(8,128)(2,1)S(1)}, u32[]{:S(2)}, u32[]{:S(2)}) collective-permute-start(bf16[8,64,128]{2,1,0:T(8,128)(2,1)S(1)} %get-tuple-element.54), channel_id=1, source_target_pairs={{0,2},{2,0},{1,3},{3,1},{4,6},{6,4},{5,7},{7,5},{8,10},{10,8},{9,1... | collective-permute-start | bytes 393224 | tf_op jit(solution)/shard_map/ppermute | solution.py:451
  60.6 0.5 collective-permute-start.13
  61.2 8.6 %collective-permute-done.12 = bf16[27,16,256]{2,1,0:T(8,128)(2,1)S(1)} collective-permute-done((bf16[27,16,256]{2,1,0:T(8,128)(2,1)S(1)}, bf16[27,16,256]{2,1,0:T(8,128)(2,1)S(1)}, u32[]{:S(2)}, u32[]{:S(2)}) %collective-permute-start.12) | collective-permute-done | bytes 221216 | tf_op jit(solution)/shard_map/ppermute | solution.py:323
  69.9 2.1 %collective-permute-start.19 = (bf16[27,16,256]{2,1,0:T(8,128)(2,1)S(1)}, bf16[27,16,256]{2,1,0:T(8,128)(2,1)S(1)}, u32[]{:S(2)}, u32[]{:S(2)}) collective-permute-start(bf16[27,16,256]{2,1,0:T(8,128)(2,1)S(1)} %collective-permute-done.12), channel_id=1, source_target_pairs={{0,4},{4,0},{8,12},{12,8},{1,5},{5,1},{9,13},{13,9},{2,6},{6,2},{1... | collective-permute-start | bytes 663560 | tf_op jit(solution)/shard_map/ppermute | solution.py:323
  72.1 1.3 %shard_map.99 = bf16[8,64,768]{2,1,0:T(8,128)(2,1)} custom-call(s32[8,768]{1,0:T(8,128)S(1)} %copy-done.3, bf16[128,768]{1,0:T(8,128)(2,1)S(1)} %get-tuple-element.53.refs_0_, bf16[128,768]{1,0:T(8,128)(2,1)S(1)} %collective-permute-done.13.refs_1_, bf16[8,64,128]{2,1,0:T(8,128)(2,1)S(1)} %get-tuple-element.44.refs_2_, ...), custom_call_target="tpu_custom_call" | custom-call | tf_op jit(solution)/shard_map/pallas_call | solution.py:456
  73.9 2.3 %collective-permute-done.22 = bf16[8,64,128]{2,1,0:T(8,128)(2,1)S(1)} collective-permute-done((bf16[8,64,128]{2,1,0:T(8,128)(2,1)S(1)}, bf16[8,64,128]{2,1,0:T(8,128)(2,1)S(1)}, u32[]{:S(2)}, u32[]{:S(2)}) %collective-permute-start.22) | collective-permute-done | bytes 131104 | tf_op jit(solution)/shard_map/ppermute | solution.py:323
  76.4 7.2 %collective-permute-done.23 = bf16[8,64,128]{2,1,0:T(8,128)(2,1)S(1)} collective-permute-done((bf16[8,64,128]{2,1,0:T(8,128)(2,1)S(1)}, bf16[8,64,128]{2,1,0:T(8,128)(2,1)S(1)}, u32[]{:S(2)}, u32[]{:S(2)}) %collective-permute-start.23) | collective-permute-done | bytes 131104 | tf_op jit(solution)/shard_map/ppermute | solution.py:323
  83.8 0.5 collective-permute-start.20
  84.5 0.6 collective-permute-done.24
  85.5 0.4 copy-done.8
  85.9 1.3 %copy-done.7 = f32[27,128,256]{2,1,0:T(8,128)} copy-done((f32[27,128,256]{2,1,0:T(8,128)}, f32[27,128,256]{2,1,0:T(8,128)S(1)}, u32[]{:S(2)}) %copy-start.7) | copy-done | bytes 3538968
  (60 shorter events, 2.3 us)
Async XLA Ops:
  0.6 16.3 %copy-start.6 = (s32[27,768]{1,0:T(8,128)S(1)}, s32[27,768]{1,0:T(8,128)}, u32[]{:S(2)}) copy-start(s32[27,768]{1,0:T(8,128)} %neighbours_ref) | copy-start | bytes 248836
  0.6 17.4 %copy-start.4 = (bf16[128,768]{1,0:T(8,128)(2,1)S(1)}, bf16[128,768]{1,0:T(8,128)(2,1)}, u32[]{:S(2)}) copy-start(bf16[128,768]{1,0:T(8,128)(2,1)} %cotangent_ref.1) | copy-start | bytes 589828
  3.4 14.7 %copy-start.5 = (bf16[768,128]{1,0:T(8,128)(2,1)S(1)}, bf16[768,128]{1,0:T(8,128)(2,1)}, u32[]{:S(2)}) copy-start(bf16[768,128]{1,0:T(8,128)(2,1)} %get-tuple-element.32.refs_0_) | copy-start | bytes 589828
  3.4 8.1 %collective-permute-start = (bf16[768,128]{1,0:T(8,128)(2,1)}, bf16[768,128]{1,0:T(8,128)(2,1)S(1)}, u32[]{:S(2)}, u32[]{:S(2)}) collective-permute-start(bf16[768,128]{1,0:T(8,128)(2,1)} %get-tuple-element.32.refs_0_), channel_id=1, source_target_pairs={{0,2},{2,0},{1,3},{3,1},{4,6},{6,4},{5,7},{7,5},{8,10},{10,8},{9,1... | collective-permute-start | bytes 589832 | tf_op jit(solution)/shard_map/ppermute | solution.py:36
  6.3 11.7 %collective-permute-start.1 = (bf16[768,128]{1,0:T(8,128)(2,1)}, bf16[768,128]{1,0:T(8,128)(2,1)S(1)}, u32[]{:S(2)}, u32[]{:S(2)}) collective-permute-start(bf16[768,128]{1,0:T(8,128)(2,1)} %get-tuple-element.32.refs_0_), channel_id=1, source_target_pairs={{1,4},{5,8},{9,12},{4,1},{8,5},{12,9},{3,6},{7,10},{11,14},{6,3},{... | collective-permute-start | bytes 589832 | tf_op jit(solution)/shard_map/ppermute | solution.py:32
  7.0 11.0 %collective-permute-start.2 = (bf16[768,128]{1,0:T(8,128)(2,1)}, bf16[768,128]{1,0:T(8,128)(2,1)S(1)}, u32[]{:S(2)}, u32[]{:S(2)}) collective-permute-start(bf16[768,128]{1,0:T(8,128)(2,1)} %get-tuple-element.32.refs_0_), channel_id=1, source_target_pairs={{0,1},{1,0},{2,3},{3,2},{4,5},{5,4},{6,7},{7,6},{8,9},{9,8},{10,11... | collective-permute-start | bytes 589832 | tf_op jit(solution)/shard_map/ppermute | solution.py:36
  11.5 6.5 %collective-permute-start.3 = (bf16[768,128]{1,0:T(8,128)(2,1)S(1)}, bf16[768,128]{1,0:T(8,128)(2,1)S(1)}, u32[]{:S(2)}, u32[]{:S(2)}) collective-permute-start(bf16[768,128]{1,0:T(8,128)(2,1)S(1)} %collective-permute-done.refs_3_), channel_id=1, source_target_pairs={{1,4},{5,8},{9,12},{4,1},{8,5},{12,9},{3,6},{7,10},{11,14},{6,3},{... | collective-permute-start | bytes 589832 | tf_op jit(solution)/shard_map/ppermute | solution.py:32
  12.2 5.9 %collective-permute-start.4 = (bf16[768,128]{1,0:T(8,128)(2,1)S(1)}, bf16[768,128]{1,0:T(8,128)(2,1)S(1)}, u32[]{:S(2)}, u32[]{:S(2)}) collective-permute-start(bf16[768,128]{1,0:T(8,128)(2,1)S(1)} %collective-permute-done.refs_3_), channel_id=1, source_target_pairs={{0,1},{1,0},{2,3},{3,2},{4,5},{5,4},{6,7},{7,6},{8,9},{9,8},{10,11... | collective-permute-start | bytes 589832 | tf_op jit(solution)/shard_map/ppermute | solution.py:36
  18.1 28.1 %copy-start.1 = (bf16[8,128,128]{2,1,0:T(8,128)(2,1)S(1)}, bf16[8,128,128]{2,1,0:T(8,128)(2,1)}, u32[]{:S(2)}) copy-start(bf16[8,128,128]{2,1,0:T(8,128)(2,1)} %weight_ref.2) | copy-start | bytes 786436
  28.2 22.7 %copy-start = (bf16[8,128,768]{2,1,0:T(8,128)(2,1)S(1)}, bf16[8,128,768]{2,1,0:T(8,128)(2,1)}, u32[]{:S(2)}) copy-start(bf16[8,128,768]{2,1,0:T(8,128)(2,1)} %children_ref.3) | copy-start | bytes 4718596
  28.2 22.7 %copy-start.2 = (f32[128,768]{1,0:T(8,128)S(1)}, f32[128,768]{1,0:T(8,128)}, u32[]{:S(2)}) copy-start(f32[128,768]{1,0:T(8,128)} %get-tuple-element.48.slope_ref) | copy-start | bytes 1179652
  28.2 22.7 %copy-start.3 = (s32[8,768]{1,0:T(8,128)S(1)}, s32[8,768]{1,0:T(8,128)}, u32[]{:S(2)}) copy-start(s32[8,768]{1,0:T(8,128)} %mask_ref.4) | copy-start | bytes 73732
  28.2 5.5 %collective-permute-start.5 = (bf16[4,27,16,256]{3,2,1,0:T(8,128)(2,1)S(1)}, bf16[4,27,16,256]{3,2,1,0:T(8,128)(2,1)S(1)}, u32[]{:S(2)}, u32[]{:S(2)}) collective-permute-start(bf16[4,27,16,256]{3,2,1,0:T(8,128)(2,1)S(1)} %get-tuple-element.39), channel_id=1, source_target_pairs={{0,1},{1,0},{2,3},{3,2},{4,5},{5,4},{6,7},{7,6},{8,9},{9,8},{10,11... | collective-permute-start | bytes 2654216 | tf_op jit(solution)/shard_map/ppermute | solution.py:36
  28.8 9.4 %collective-permute-start.6 = (bf16[768,128]{1,0:T(8,128)(2,1)S(1)}, bf16[768,128]{1,0:T(8,128)(2,1)S(1)}, u32[]{:S(2)}, u32[]{:S(2)}) collective-permute-start(bf16[768,128]{1,0:T(8,128)(2,1)S(1)} %get-tuple-element.41.refs_0_), channel_id=1, source_target_pairs={{1,4},{5,8},{9,12},{4,1},{8,5},{12,9},{3,6},{7,10},{11,14},{6,3},{... | collective-permute-start | bytes 589832 | tf_op jit(solution)/shard_map/ppermute | solution.py:32
  29.7 8.6 %collective-permute-start.7 = (bf16[768,128]{1,0:T(8,128)(2,1)S(1)}, bf16[768,128]{1,0:T(8,128)(2,1)S(1)}, u32[]{:S(2)}, u32[]{:S(2)}) collective-permute-start(bf16[768,128]{1,0:T(8,128)(2,1)S(1)} %get-tuple-element.41.refs_0_), channel_id=1, source_target_pairs={{0,1},{1,0},{2,3},{3,2},{4,5},{5,4},{6,7},{7,6},{8,9},{9,8},{10,11... | collective-permute-start | bytes 589832 | tf_op jit(solution)/shard_map/ppermute | solution.py:36
  33.9 19.2 %collective-permute-start.10 = (bf16[27,16,256]{2,1,0:T(8,128)(2,1)S(1)}, bf16[27,16,256]{2,1,0:T(8,128)(2,1)S(1)}, u32[]{:S(2)}, u32[]{:S(2)}) collective-permute-start(bf16[27,16,256]{2,1,0:T(8,128)(2,1)S(1)} %get-tuple-element.64), channel_id=1, source_target_pairs={{0,8},{4,12},{8,0},{12,4},{1,9},{5,13},{9,1},{13,5},{2,10},{6,14},... | collective-permute-start | bytes 663560 | tf_op jit(solution)/shard_map/ppermute | solution.py:323
  36.5 16.7 %collective-permute-start.11 = (bf16[27,16,256]{2,1,0:T(8,128)(2,1)S(1)}, bf16[27,16,256]{2,1,0:T(8,128)(2,1)S(1)}, u32[]{:S(2)}, u32[]{:S(2)}) collective-permute-start(bf16[27,16,256]{2,1,0:T(8,128)(2,1)S(1)} %get-tuple-element.63), channel_id=1, source_target_pairs={{0,12},{4,8},{8,4},{12,0},{1,13},{5,9},{9,5},{13,1},{2,14},{6,10},... | collective-permute-start | bytes 663560 | tf_op jit(solution)/shard_map/ppermute | solution.py:323
  38.2 15.0 %collective-permute-start.9 = (bf16[27,16,256]{2,1,0:T(8,128)(2,1)S(1)}, bf16[27,16,256]{2,1,0:T(8,128)(2,1)S(1)}, u32[]{:S(2)}, u32[]{:S(2)}) collective-permute-start(bf16[27,16,256]{2,1,0:T(8,128)(2,1)S(1)} %get-tuple-element.65), channel_id=1, source_target_pairs={{0,4},{4,0},{8,12},{12,8},{1,5},{5,1},{9,13},{13,9},{2,6},{6,2},{1... | collective-permute-start | bytes 663560 | tf_op jit(solution)/shard_map/ppermute | solution.py:323
  44.6 6.3 %collective-permute-start.8 = (bf16[128,768]{1,0:T(8,128)(2,1)S(1)}, bf16[128,768]{1,0:T(8,128)(2,1)S(1)}, u32[]{:S(2)}, u32[]{:S(2)}) collective-permute-start(bf16[128,768]{1,0:T(8,128)(2,1)S(1)} %bitcast.9), channel_id=1, source_target_pairs={{0,2},{2,0},{1,3},{3,1},{4,6},{6,4},{5,7},{7,5},{8,10},{10,8},{9,1... | collective-permute-start | bytes 589832 | tf_op jit(solution)/shard_map/ppermute | solution.py:413
  53.3 7.3 %collective-permute-start.21 = (bf16[8,64,128]{2,1,0:T(8,128)(2,1)S(1)}, bf16[8,64,128]{2,1,0:T(8,128)(2,1)S(1)}, u32[]{:S(2)}, u32[]{:S(2)}) collective-permute-start(bf16[8,64,128]{2,1,0:T(8,128)(2,1)S(1)} %get-tuple-element.58), channel_id=1, source_target_pairs={{0,1},{1,0},{2,3},{3,2},{4,5},{5,4},{6,7},{7,6},{8,9},{9,8},{10,11... | collective-permute-start | bytes 393224 | tf_op jit(solution)/shard_map/ppermute | solution.py:36
  53.4 16.4 %collective-permute-start.12 = (bf16[27,16,256]{2,1,0:T(8,128)(2,1)S(1)}, bf16[27,16,256]{2,1,0:T(8,128)(2,1)S(1)}, u32[]{:S(2)}, u32[]{:S(2)}) collective-permute-start(bf16[27,16,256]{2,1,0:T(8,128)(2,1)S(1)} %add_convert_fusion), channel_id=1, source_target_pairs={{0,8},{4,12},{8,0},{12,4},{1,9},{5,13},{9,1},{13,5},{2,10},{6,14},... | collective-permute-start | bytes 663560 | tf_op jit(solution)/shard_map/ppermute | solution.py:323
  59.0 14.8 %collective-permute-start.15 = (bf16[27,16,256]{2,1,0:T(8,128)(2,1)S(1)}, bf16[27,16,256]{2,1,0:T(8,128)(2,1)S(1)}, u32[]{:S(2)}, u32[]{:S(2)}) collective-permute-start(bf16[27,16,256]{2,1,0:T(8,128)(2,1)S(1)} %add_convert_fusion), channel_id=1, source_target_pairs={{0,1},{1,0},{2,3},{3,2},{4,5},{5,4},{6,7},{7,6},{8,9},{9,8},{10,11... | collective-permute-start | bytes 663560 | tf_op jit(solution)/shard_map/ppermute | solution.py:36
  59.1 12.8 %collective-permute-start.16 = (bf16[27,16,256]{2,1,0:T(8,128)(2,1)S(1)}, bf16[27,16,256]{2,1,0:T(8,128)(2,1)S(1)}, u32[]{:S(2)}, u32[]{:S(2)}) collective-permute-start(bf16[27,16,256]{2,1,0:T(8,128)(2,1)S(1)} %add_convert_fusion), channel_id=1, source_target_pairs={{0,4},{4,0},{8,12},{12,8},{1,5},{5,1},{9,13},{13,9},{2,6},{6,2},{1... | collective-permute-start | bytes 663560 | tf_op jit(solution)/shard_map/ppermute | solution.py:323
  59.1 10.7 %collective-permute-start.14 = (bf16[8,64,128]{2,1,0:T(8,128)(2,1)S(1)}, bf16[8,64,128]{2,1,0:T(8,128)(2,1)S(1)}, u32[]{:S(2)}, u32[]{:S(2)}) collective-permute-start(bf16[8,64,128]{2,1,0:T(8,128)(2,1)S(1)} %get-tuple-element.54), channel_id=1, source_target_pairs={{0,2},{2,0},{1,3},{3,1},{4,6},{6,4},{5,7},{7,5},{8,10},{10,8},{9,1... | collective-permute-start | bytes 393224 | tf_op jit(solution)/shard_map/ppermute | solution.py:451
  60.6 9.2 %collective-permute-start.13 = (bf16[128,768]{1,0:T(8,128)(2,1)S(1)}, bf16[128,768]{1,0:T(8,128)(2,1)S(1)}, u32[]{:S(2)}, u32[]{:S(2)}) collective-permute-start(bf16[128,768]{1,0:T(8,128)(2,1)S(1)} %get-tuple-element.53.refs_0_), channel_id=1, source_target_pairs={{0,2},{2,0},{1,3},{3,1},{4,6},{6,4},{5,7},{7,5},{8,10},{10,8},{9,1... | collective-permute-start | bytes 589832 | tf_op jit(solution)/shard_map/ppermute | solution.py:445
  69.8 6.4 %collective-permute-start.22 = (bf16[8,64,128]{2,1,0:T(8,128)(2,1)S(1)}, bf16[8,64,128]{2,1,0:T(8,128)(2,1)S(1)}, u32[]{:S(2)}, u32[]{:S(2)}) collective-permute-start(bf16[8,64,128]{2,1,0:T(8,128)(2,1)S(1)} %add_convert_fusion.7), channel_id=1, source_target_pairs={{0,4},{4,0},{8,12},{12,8},{1,5},{5,1},{9,13},{13,9},{2,6},{6,2},{1... | collective-permute-start | bytes 393224 | tf_op jit(solution)/shard_map/ppermute | solution.py:323
  69.8 14.5 %collective-permute-start.18 = (bf16[27,16,256]{2,1,0:T(8,128)(2,1)S(1)}, bf16[27,16,256]{2,1,0:T(8,128)(2,1)S(1)}, u32[]{:S(2)}, u32[]{:S(2)}) collective-permute-start(bf16[27,16,256]{2,1,0:T(8,128)(2,1)S(1)} %collective-permute-done.12), channel_id=1, source_target_pairs={{0,1},{1,0},{2,3},{3,2},{4,5},{5,4},{6,7},{7,6},{8,9},{9,8},{10,11... | collective-permute-start | bytes 663560 | tf_op jit(solution)/shard_map/ppermute | solution.py:36
  69.9 13.9 %collective-permute-start.19 = (bf16[27,16,256]{2,1,0:T(8,128)(2,1)S(1)}, bf16[27,16,256]{2,1,0:T(8,128)(2,1)S(1)}, u32[]{:S(2)}, u32[]{:S(2)}) collective-permute-start(bf16[27,16,256]{2,1,0:T(8,128)(2,1)S(1)} %collective-permute-done.12), channel_id=1, source_target_pairs={{0,4},{4,0},{8,12},{12,8},{1,5},{5,1},{9,13},{13,9},{2,6},{6,2},{1... | collective-permute-start | bytes 663560 | tf_op jit(solution)/shard_map/ppermute | solution.py:323
  71.9 12.3 %collective-permute-start.17 = (bf16[27,16,256]{2,1,0:T(8,128)(2,1)S(1)}, bf16[27,16,256]{2,1,0:T(8,128)(2,1)S(1)}, u32[]{:S(2)}, u32[]{:S(2)}) collective-permute-start(bf16[27,16,256]{2,1,0:T(8,128)(2,1)S(1)} %collective-permute-done.16), channel_id=1, source_target_pairs={{0,1},{1,0},{2,3},{3,2},{4,5},{5,4},{6,7},{7,6},{8,9},{9,8},{10,11... | collective-permute-start | bytes 663560 | tf_op jit(solution)/shard_map/ppermute | solution.py:36
  76.3 7.3 %collective-permute-start.23 = (bf16[8,64,128]{2,1,0:T(8,128)(2,1)S(1)}, bf16[8,64,128]{2,1,0:T(8,128)(2,1)S(1)}, u32[]{:S(2)}, u32[]{:S(2)}) collective-permute-start(bf16[8,64,128]{2,1,0:T(8,128)(2,1)S(1)} %add_convert_fusion.6), channel_id=1, source_target_pairs={{0,8},{4,12},{8,0},{12,4},{1,9},{5,13},{9,1},{13,5},{2,10},{6,14},... | collective-permute-start | bytes 393224 | tf_op jit(solution)/shard_map/ppermute | solution.py:323
  83.7 1.4 %collective-permute-start.24 = (bf16[8,64,128]{2,1,0:T(8,128)(2,1)S(1)}, bf16[8,64,128]{2,1,0:T(8,128)(2,1)S(1)}, u32[]{:S(2)}, u32[]{:S(2)}) collective-permute-start(bf16[8,64,128]{2,1,0:T(8,128)(2,1)S(1)} %get-tuple-element.61), channel_id=1, source_target_pairs={{0,1},{1,0},{2,3},{3,2},{4,5},{5,4},{6,7},{7,6},{8,9},{9,8},{10,11... | collective-permute-start | bytes 393224 | tf_op jit(solution)/shard_map/ppermute | solution.py:36
  83.8 1.6 %collective-permute-start.20 = (bf16[27,16,256]{2,1,0:T(8,128)(2,1)S(1)}, bf16[27,16,256]{2,1,0:T(8,128)(2,1)S(1)}, u32[]{:S(2)}, u32[]{:S(2)}) collective-permute-start(bf16[27,16,256]{2,1,0:T(8,128)(2,1)S(1)} %collective-permute-done.19), channel_id=1, source_target_pairs={{0,1},{1,0},{2,3},{3,2},{4,5},{5,4},{6,7},{7,6},{8,9},{9,8},{10,11... | collective-permute-start | bytes 663560 | tf_op jit(solution)/shard_map/ppermute | solution.py:36
  (2 other events, 2.6 us)
where the time goes:
time: 87.6 us; the launch traced here: 87.3 us
  starting transfers between devices  32.4 us (37%)
  waiting for transfers between devices  26.2 us (30%)
  Pallas kernels  22.9 us (26%)
  other arithmetic  2.45 us (3%)
  local copies, waits for them, and re-layouts  2.24 us (3%)
  between operations  1.05 us (1%)
    ppermute x8, waiting for transfers between devices, apart(): lax.ppermute(shard, 'curve', [(i, i ^ by) for i in range(lax.axis_size('c...  19.2 us
    ppermute x11, starting transfers between devices, swapped(): return lax.ppermute(shard, axis, [(0, 1), (1, 0)])  14.6 us
    ppermute x8, starting transfers between devices, apart(): lax.ppermute(shard, 'curve', [(i, i ^ by) for i in range(lax.axis_size('c...  12 us
    pallas_call x1, Pallas kernels, body(): call(functools.partial(conv_kernel, chans, shards, scale), [shape((channe...  10.1 us
    pallas_call x1, Pallas kernels, body(): call(coarse_grad_kernel, [shape((channels, rows), F32), shape((chans - 1,...  6.35 us
    ppermute x1, waiting for transfers between devices, body(): lax.ppermute(others[by - 1], 'chan', [(i, (i + by) % chans) for i in rang...  4.6 us
    pallas_call x1, Pallas kernels, body(): call(down_kernel, [shape((rows, channels), BF16), shape((channels, rows),...  2.74 us
    ppermute x11, waiting for transfers between devices, swapped(): return lax.ppermute(shard, axis, [(0, 1), (1, 0)])  2.43 us
  transfers between devices with their start and end apart: 25, of which 8 were waited for; matrix products, arithmetic and copies ran while one was open for 3% of the time, Pallas kernels for 12%

commit v1 on v0

--- a/solution.py
+++ b/solution.py
@@ -173,8 +173,8 @@
 
 def conv_kernel(chans, shards, scale, scalars_ref, index_ref, weight_ref, cotangent_ref, *refs):
     parts, refs = [refs[3 * i : 3 * i + 3] for i in range(chans)], refs[3 * chans :]
-    out_ref, grad_ref, keep_ref, send_ref = refs[:4]
-    window_ref, column_ref, picked_ref, conv_ref, scratch_ref = refs[4:]
+    out_ref, grad_ref, keep_ref, send_ref, far_ref = refs[:5]
+    window_ref, column_ref, picked_ref, conv_ref, scratch_ref = refs[5:]
     rows = index_ref.shape[2]
     blocks = rows // BLOCK
     width = chans * window_ref.shape[2]
@@ -220,7 +220,11 @@
             for step in range(shards):
                 at = step * size
                 keep_ref[step, three * 3 + j] = both[at : at + size]
-                send_ref[step, three * 3 + j] = both[half + at : half + at + size]
+                other = both[half + at : half + at + size]
+                if step == shards - 1:
+                    far_ref[three * 3 + j] = other
+                if step < send_ref.shape[0]:
+                    send_ref[step, three * 3 + j] = other
         return 0
 
     lax.fori_loop(0, 9, weigh, 0, unroll=3)
@@ -327,13 +331,6 @@
     return sum(term.astype(F32) for term in terms).astype(BF16)
 
 
-def sum_over_curve(total, beside):
-    terms = [apart(total[by], by) for by in range(1, 4)]
-    own = added(after(total[0], beside), *terms)
-    across = apart(own, 2)
-    return [own, apart(own, 1), across, apart(across, 1)]
-
-
 def after(value, *earlier):
     return lax.optimization_barrier((value, *earlier))[0]
 
@@ -376,13 +373,14 @@
         vmem(1) + SMEM,
     )(after(neighbours, parts[1]))
 
-    features_out, conv_grad, keep, send = call(
+    features_out, conv_grad, keep, send, far = call(
         functools.partial(conv_kernel, chans, shards, scale),
         [
             shape((channels, rows), BF16),
             shape((rows, channels), BF16),
             shape((shards, offsets, size, width), BF16),
-            shape((shards, offsets, size, width), BF16),
+            shape((max(shards - 1, 1), offsets, size, width), BF16),
+            shape((offsets, size, width), BF16),
         ],
         SMEM + vmem(3 + 3 * chans),
         [
@@ -394,9 +392,16 @@
         ],
     )(scalars, index, conv_weight, cotangent, *windows)
 
-    near = met(conv_grad)
-    received = swapped(send, "rep")
-    total = [added(keep[i], received[i]) for i in range(shards)]
+    far = added(keep[shards - 1], swapped(far, "rep"))
+    first = far
+    if shards == 4:
+        received = swapped(after(send, far), "rep")
+        total = [added(keep[i], received[i]) for i in range(3)]
+        near = met(after(conv_grad, total[2]))
+        first = added(after(total[2], *near), apart(far, 1))
+        terms = [apart(first, 2), apart(after(total[1], first), 1)]
+    else:
+        near = met(conv_grad)
 
     mine, others = call(
         coarse_grad_kernel,
@@ -408,7 +413,7 @@
             pltpu.VMEM((GROUPS, rows, PER * channels), BF16),
             pltpu.VMEM((chans, channels, rows), F32),
         ],
-    )(after(scalars, *total), index, conv_weight, conv_grad, *near)
+    )(after(scalars, first), index, conv_weight, conv_grad, *near)
     received = [
         lax.ppermute(others[by - 1], "chan", [(i, (i + by) % chans) for i in range(chans)])
         for by in range(1, chans)
@@ -436,11 +441,13 @@
     )(after(scalars, *cut, *blank), children, child_mask, slope, mine, *received)
 
     if shards == 4:
-        sums = sum_over_curve(total, pre_grad)
+        own = added(after(total[0], pre_grad), *terms)
+        across = apart(own, 2)
+        sums = [own, apart(own, 1), across, apart(across, 1)]
     else:
-        sums = [lax.psum(total[0], "curve")]
-    own = sums[0]
-    sent_grad, send = after(pre_grad, own), after(send, own)
+        own = lax.psum(far, "curve")
+        sums = [own]
+    sent_grad = after(pre_grad, own)
     grads = [
         lax.ppermute(sent_grad, "chan", [(i, (i + by) % chans) for i in range(chans)])
         if by
@@ -459,12 +466,12 @@
         vmem(1 + 2 * chans),
         [pltpu.VMEM((octants, mine_fine, rows), BF16), pltpu.SemaphoreType.DMA((octants,))],
         anywhere(1)[0],
-    )(after(child_mask, *sums[2:3]), *grads, *weights)
+    )(child_mask, *grads, *weights)
 
     down = added(keep, swapped(send, "rep"))
     if shards == 4:
-        down = added(down, apart(down, 1))
-        down = added(after(down, children_grad), apart(down, 2))
+        down = added(after(down, sums[2], children_grad), apart(down, 1))
+        down = added(down, apart(down, 2))
     else:
         down = lax.psum(down, "curve")
     def joined(result, pieces):
@@ -477,7 +484,7 @@
     pieces = []
     for step, part in enumerate(sums):
         at = (curve ^ step) * size if shards > 1 else 0
-        mine = part if step else after(part, *sums[2:3])
+        mine = part if step else after(part, *grads[1:])
         pieces += [(rows_of[0] + at, mine), (rows_of[1] + at, swapped(part, "rep"))]
     conv_weight_grad = joined(blank[0], pieces)
     return (features_out, children_grad, conv_weight_grad, down_weight_grad)

time: 87.6 us -> 90.3 us (1.031)
  other arithmetic: 2.45 us -> 4.8 us
  waiting for transfers between devices: 26.2 us -> 24.2 us
  starting transfers between devices: 32.4 us -> 34.2 us
    ppermute x8, waiting for transfers between devices: 19.2 us -> 7.37 us  [apart(): lax.ppermute(shard, 'curve', [(i, i ^ by) for i in range(lax.axis_size('c...]
    ppermute x1, waiting for transfers between devices: 0.01 us -> 7.74 us  [body(): lax.ppermute(sent_grad, 'chan', [(i, (i + by) % chans) for i in range(cha...]
    ppermute x11 -> x12, waiting for transfers between devices: 2.43 us -> 4.91 us  [swapped(): return lax.ppermute(shard, axis, [(0, 1), (1, 0)])]
    convert_element_type x4 -> x6, other arithmetic: 0.44 us -> 2.81 us  [added(): return sum((term.astype(F32) for term in terms)).astype(BF16)]
    ppermute x8, starting transfers between devices: 12 us -> 14 us  [apart(): lax.ppermute(shard, 'curve', [(i, i ^ by) for i in range(lax.axis_size('c...]
    ppermute x11 -> x12, starting transfers between devices: 14.6 us -> 14.5 us  [swapped(): return lax.ppermute(shard, axis, [(0, 1), (1, 0)])]
  transfers between devices with their start and end apart: 25 -> 26, of which waited for: 8 -> 9; matrix products, arithmetic and copies ran while one was open for 3% -> 5% of each run, Pallas kernels for 12% -> 12%
where the time goes in v1:
time: 90.3 us; the launch traced here: 90.1 us
  starting transfers between devices  34.2 us (38%)
  waiting for transfers between devices  24.2 us (27%)
  Pallas kernels  23.6 us (26%)
  other arithmetic  4.8 us (5%)
  local copies, waits for them, and re-layouts  2.23 us (2%)
  between operations  0.99 us (1%)
    ppermute x12, starting transfers between devices, swapped(): return lax.ppermute(shard, axis, [(0, 1), (1, 0)])  14.5 us
    ppermute x8, starting transfers between devices, apart(): lax.ppermute(shard, 'curve', [(i, i ^ by) for i in range(lax.axis_size('c...  14 us
    pallas_call x1, Pallas kernels, body(): call(functools.partial(conv_kernel, chans, shards, scale), [shape((channe...  10.5 us
    ppermute x1, waiting for transfers between devices, body(): lax.ppermute(sent_grad, 'chan', [(i, (i + by) % chans) for i in range(cha...  7.74 us
    ppermute x8, waiting for transfers between devices, apart(): lax.ppermute(shard, 'curve', [(i, i ^ by) for i in range(lax.axis_size('c...  7.37 us
    pallas_call x1, Pallas kernels, body(): call(coarse_grad_kernel, [shape((channels, rows), F32), shape((chans - 1,...  6.72 us
    ppermute x12, waiting for transfers between devices, swapped(): return lax.ppermute(shard, axis, [(0, 1), (1, 0)])  4.91 us
    ppermute x1, waiting for transfers between devices, body(): lax.ppermute(others[by - 1], 'chan', [(i, (i + by) % chans) for i in rang...  4.18 us
  transfers between devices with their start and end apart: 26, of which 9 were waited for; matrix products, arithmetic and copies ran while one was open for 5% of the time, Pallas kernels for 12%

profile of v1, /device:TPU:0, one launch (start us, length us, event | category | flops | bytes accessed | tf_op | source)
XLA Modules:
  0.0 90.1 jit_solution(1240276712383547236)
XLA Ops:
  0.7 2.7 %shard_map.93 = (bf16[768,128]{1,0:T(8,128)(2,1)}, f32[128,768]{1,0:T(8,128)}) custom-call(bf16[8,128,768]{2,1,0:T(8,128)(2,1)} %children_ref.3, s32[8,768]{1,0:T(8,128)} %mask_ref.5, bf16[8,128,128]{2,1,0:T(8,128)(2,1)} %weight_ref.2), custom_call_target="tpu_custom_call" | custom-call | tf_op jit(solution)/shard_map/pallas_call | solution.py:353
  3.4 2.9 %collective-permute-start = (bf16[768,128]{1,0:T(8,128)(2,1)}, bf16[768,128]{1,0:T(8,128)(2,1)S(1)}, u32[]{:S(2)}, u32[]{:S(2)}) collective-permute-start(bf16[768,128]{1,0:T(8,128)(2,1)} %get-tuple-element.35.refs_0_), channel_id=1, source_target_pairs={{0,2},{2,0},{1,3},{3,1},{4,6},{6,4},{5,7},{7,5},{8,10},{10,8},{9,1... | collective-permute-start | bytes 589832 | tf_op jit(solution)/shard_map/ppermute | solution.py:36
  7.0 3.0 %collective-permute-start.2 = (bf16[768,128]{1,0:T(8,128)(2,1)}, bf16[768,128]{1,0:T(8,128)(2,1)S(1)}, u32[]{:S(2)}, u32[]{:S(2)}) collective-permute-start(bf16[768,128]{1,0:T(8,128)(2,1)} %get-tuple-element.35.refs_0_), channel_id=1, source_target_pairs={{0,1},{1,0},{2,3},{3,2},{4,5},{5,4},{6,7},{7,6},{8,9},{9,8},{10,11... | collective-permute-start | bytes 589832 | tf_op jit(solution)/shard_map/ppermute | solution.py:36
  10.0 1.5 %collective-permute-done.refs_3_ = bf16[768,128]{1,0:T(8,128)(2,1)S(1)} collective-permute-done((bf16[768,128]{1,0:T(8,128)(2,1)}, bf16[768,128]{1,0:T(8,128)(2,1)S(1)}, u32[]{:S(2)}, u32[]{:S(2)}) %collective-permute-start) | collective-permute-done | bytes 196640 | tf_op jit(solution)/shard_map/ppermute | solution.py:36
  12.2 3.2 %collective-permute-start.4 = (bf16[768,128]{1,0:T(8,128)(2,1)S(1)}, bf16[768,128]{1,0:T(8,128)(2,1)S(1)}, u32[]{:S(2)}, u32[]{:S(2)}) collective-permute-start(bf16[768,128]{1,0:T(8,128)(2,1)S(1)} %collective-permute-done.refs_3_), channel_id=1, source_target_pairs={{0,1},{1,0},{2,3},{3,2},{4,5},{5,4},{6,7},{7,6},{8,9},{9,8},{10,11... | collective-permute-start | bytes 589832 | tf_op jit(solution)/shard_map/ppermute | solution.py:36
  15.3 1.6 %broadcast_multiply_fusion.weight_ref = bf16[27,128,256]{2,1,0:T(8,128)(2,1)S(1)} fusion(bf16[27,128,256]{2,1,0:T(8,128)(2,1)} %param.10, bf16[]{:T(256)} %constant.3.clone.1), kind=kLoop, calls=%fused_computation | loop fusion | flops 884736 | bytes 3538946 | tf_op jit(solution)/shard_map/mul | solution.py:367
  17.0 1.0 %shard_map.94 = (s32[3,16,768]{2,1,0:T(8,128)S(1)}, s32[39]{0:T(128)S(1)}) custom-call(s32[27,768]{1,0:T(8,128)S(1)} %copy-done.6), custom_call_target="tpu_custom_call" | custom-call | tf_op jit(solution)/shard_map/pallas_call | solution.py:368
  18.1 10.5 %shard_map.95 = (bf16[128,768]{1,0:T(8,128)(2,1)}, bf16[768,128]{1,0:T(8,128)(2,1)S(1)}, bf16[4,27,16,256]{3,2,1,0:T(8,128)(2,1)S(1)}, bf16[3,27,16,256]{3,2,1,0:T(8,128)(2,1)S(1)}, bf16[27,16,256]{2,1,0:T(8,128)(2,1)S(1)}) custom-call(s32[39]{0:T(128)S(1)} %get-tuple-element.54.scalars_ref, s32[3,16,768]{2,1,0:T(8,128)S(1)} %get-tuple-element.38.index_ref, ...), custom_call_target="tpu_custom_call" | custom-call | tf_op jit(solution)/shard_map/pallas_call | solution.py:376
  28.5 1.0 %collective-permute-start.5 = (bf16[27,16,256]{2,1,0:T(8,128)(2,1)S(1)}, bf16[27,16,256]{2,1,0:T(8,128)(2,1)S(1)}, u32[]{:S(2)}, u32[]{:S(2)}) collective-permute-start(bf16[27,16,256]{2,1,0:T(8,128)(2,1)S(1)} %get-tuple-element.43), channel_id=1, source_target_pairs={{0,1},{1,0},{2,3},{3,2},{4,5},{5,4},{6,7},{7,6},{8,9},{9,8},{10,11... | collective-permute-start | bytes 663560 | tf_op jit(solution)/shard_map/ppermute | solution.py:36
  29.5 1.1 %collective-permute-done.5 = bf16[27,16,256]{2,1,0:T(8,128)(2,1)S(1)} collective-permute-done((bf16[27,16,256]{2,1,0:T(8,128)(2,1)S(1)}, bf16[27,16,256]{2,1,0:T(8,128)(2,1)S(1)}, u32[]{:S(2)}, u32[]{:S(2)}) %collective-permute-start.5) | collective-permute-done | bytes 221216 | tf_op jit(solution)/shard_map/ppermute | solution.py:36
  31.2 1.8 %collective-permute-start.9 = (bf16[27,16,256]{2,1,0:T(8,128)(2,1)S(1)}, bf16[27,16,256]{2,1,0:T(8,128)(2,1)S(1)}, u32[]{:S(2)}, u32[]{:S(2)}) collective-permute-start(bf16[27,16,256]{2,1,0:T(8,128)(2,1)S(1)} %fusion), channel_id=1, source_target_pairs={{0,4},{4,0},{8,12},{12,8},{1,5},{5,1},{9,13},{13,9},{2,6},{6,2},{1... | collective-permute-start | bytes 663560 | tf_op jit(solution)/shard_map/ppermute | solution.py:327
  32.9 0.9 fusion.2
  33.8 0.8 collective-permute-start.7
  34.7 3.4 %collective-permute-start.8 = (bf16[768,128]{1,0:T(8,128)(2,1)S(1)}, bf16[768,128]{1,0:T(8,128)(2,1)S(1)}, u32[]{:S(2)}, u32[]{:S(2)}) collective-permute-start(bf16[768,128]{1,0:T(8,128)(2,1)S(1)} %get-tuple-element.46.refs_0_), channel_id=1, source_target_pairs={{0,1},{1,0},{2,3},{3,2},{4,5},{5,4},{6,7},{7,6},{8,9},{9,8},{10,11... | collective-permute-start | bytes 589832 | tf_op jit(solution)/shard_map/ppermute | solution.py:36
  38.0 1.1 %collective-permute-done.8.refs_2_ = bf16[768,128]{1,0:T(8,128)(2,1)S(1)} collective-permute-done((bf16[768,128]{1,0:T(8,128)(2,1)S(1)}, bf16[768,128]{1,0:T(8,128)(2,1)S(1)}, u32[]{:S(2)}, u32[]{:S(2)}) %collective-permute-start.8) | collective-permute-done | bytes 196640 | tf_op jit(solution)/shard_map/ppermute | solution.py:36
  39.9 3.6 %collective-permute-start.12 = (bf16[27,16,256]{2,1,0:T(8,128)(2,1)}, bf16[27,16,256]{2,1,0:T(8,128)(2,1)S(1)}, u32[]{:S(2)}, u32[]{:S(2)}) collective-permute-start(bf16[27,16,256]{2,1,0:T(8,128)(2,1)} %get-tuple-element.59), channel_id=1, source_target_pairs={{0,4},{4,0},{8,12},{12,8},{1,5},{5,1},{9,13},{13,9},{2,6},{6,2},{1... | collective-permute-start | bytes 663560 | tf_op jit(solution)/shard_map/ppermute | solution.py:327
  43.5 2.2 %collective-permute-start.11 = (bf16[27,16,256]{2,1,0:T(8,128)(2,1)}, bf16[27,16,256]{2,1,0:T(8,128)(2,1)}, u32[]{:S(2)}, u32[]{:S(2)}) collective-permute-start(bf16[27,16,256]{2,1,0:T(8,128)(2,1)} %add_convert_fusion.3), channel_id=1, source_target_pairs={{0,8},{4,12},{8,0},{12,4},{1,9},{5,13},{9,1},{13,5},{2,10},{6,14},... | collective-permute-start | bytes 663560 | tf_op jit(solution)/shard_map/ppermute | solution.py:327
  45.7 6.7 %shard_map.96 = (f32[128,768]{1,0:T(8,128)S(1)}, bf16[1,128,768]{2,1,0:T(8,128)(2,1)S(1)}) custom-call(s32[39]{0:T(128)S(1)} %get-tuple-element.54.scalars_ref, s32[3,16,768]{2,1,0:T(8,128)S(1)} %get-tuple-element.38.index_ref, bf16[27,128,256]{2,1,0:T(8,128)(2,1)S(1)} %broadcast_multiply_fusion.weight_ref, bf16[768,128]{1,0:T(8,128)(2,1)S(1)} %get-tuple-element.46.refs_0_, ...), custom_call_target="tpu_custom_call" | custom-call | tf_op jit(solution)/shard_map/pallas_call | solution.py:406
  52.5 1.5 %collective-permute-start.10 = (bf16[128,768]{1,0:T(8,128)(2,1)S(1)}, bf16[128,768]{1,0:T(8,128)(2,1)S(1)}, u32[]{:S(2)}, u32[]{:S(2)}) collective-permute-start(bf16[128,768]{1,0:T(8,128)(2,1)S(1)} %bitcast.10), channel_id=1, source_target_pairs={{0,2},{2,0},{1,3},{3,1},{4,6},{6,4},{5,7},{7,5},{8,10},{10,8},{9,1... | collective-permute-start | bytes 589832 | tf_op jit(solution)/shard_map/ppermute | solution.py:418
  54.2 4.2 %collective-permute-done.10.refs_0_ = bf16[128,768]{1,0:T(8,128)(2,1)S(1)} collective-permute-done((bf16[128,768]{1,0:T(8,128)(2,1)S(1)}, bf16[128,768]{1,0:T(8,128)(2,1)S(1)}, u32[]{:S(2)}, u32[]{:S(2)}) %collective-permute-start.10) | collective-permute-done | bytes 196640 | tf_op jit(solution)/shard_map/ppermute | solution.py:418
  58.4 1.2 %shard_map.98 = (bf16[128,768]{1,0:T(8,128)(2,1)S(1)}, bf16[8,64,128]{2,1,0:T(8,128)(2,1)S(1)}, bf16[8,64,128]{2,1,0:T(8,128)(2,1)S(1)}) custom-call(s32[39]{0:T(128)S(1)} %get-tuple-element.54.scalars_ref, bf16[8,128,768]{2,1,0:T(8,128)(2,1)S(1)} %copy-done, s32[8,768]{1,0:T(8,128)S(1)} %copy-done.3, f32[128,768]{1,0:T(8,128)S(1)} %copy-done.2, ...), custom_call_target="tpu_custom_call" | custom-call | tf_op jit(solution)/shard_map/pallas_call | solution.py:432
  59.7 1.0 %add_convert_fusion = bf16[27,16,256]{2,1,0:T(8,128)(2,1)S(1)} fusion(bf16[27,16,256]{2,1,0:T(8,128)(2,1)S(1)} %collective-permute-done.12, bf16[27,16,256]{2,1,0:T(8,128)(2,1)} %collective-permute-done.11, bf16[27,16,256]{2,1,0:T(8,128)(2,1)S(1)} %get-tuple-element.58), kind=kLoop, calls=%fused_computation.11 | loop fusion | flops 663552 | bytes 884736 | tf_op jit(solution)/shard_map/convert_element_type | solution.py:331
  60.7 1.7 %collective-permute-start.18 = (bf16[27,16,256]{2,1,0:T(8,128)(2,1)S(1)}, bf16[27,16,256]{2,1,0:T(8,128)(2,1)S(1)}, u32[]{:S(2)}, u32[]{:S(2)}) collective-permute-start(bf16[27,16,256]{2,1,0:T(8,128)(2,1)S(1)} %add_convert_fusion), channel_id=1, source_target_pairs={{0,8},{4,12},{8,0},{12,4},{1,9},{5,13},{9,1},{13,5},{2,10},{6,14},... | collective-permute-start | bytes 663560 | tf_op jit(solution)/shard_map/ppermute | solution.py:327
  62.7 1.5 %collective-permute-start.14 = (bf16[8,64,128]{2,1,0:T(8,128)(2,1)S(1)}, bf16[8,64,128]{2,1,0:T(8,128)(2,1)S(1)}, u32[]{:S(2)}, u32[]{:S(2)}) collective-permute-start(bf16[8,64,128]{2,1,0:T(8,128)(2,1)S(1)} %get-tuple-element.61), channel_id=1, source_target_pairs={{0,2},{2,0},{1,3},{3,1},{4,6},{6,4},{5,7},{7,5},{8,10},{10,8},{9,1... | collective-permute-start | bytes 393224 | tf_op jit(solution)/shard_map/ppermute | solution.py:458
  64.8 7.7 %collective-permute-done.13.refs_1_ = bf16[128,768]{1,0:T(8,128)(2,1)S(1)} collective-permute-done((bf16[128,768]{1,0:T(8,128)(2,1)S(1)}, bf16[128,768]{1,0:T(8,128)(2,1)S(1)}, u32[]{:S(2)}, u32[]{:S(2)}) %collective-permute-start.13) | collective-permute-done | bytes 196640 | tf_op jit(solution)/shard_map/ppermute | solution.py:452
  72.5 1.7 %collective-permute-start.23 = (bf16[8,64,128]{2,1,0:T(8,128)(2,1)S(1)}, bf16[8,64,128]{2,1,0:T(8,128)(2,1)S(1)}, u32[]{:S(2)}, u32[]{:S(2)}) collective-permute-start(bf16[8,64,128]{2,1,0:T(8,128)(2,1)S(1)} %add_convert_fusion.7), channel_id=1, source_target_pairs={{0,4},{4,0},{8,12},{12,8},{1,5},{5,1},{9,13},{13,9},{2,6},{6,2},{1... | collective-permute-start | bytes 393224 | tf_op jit(solution)/shard_map/ppermute | solution.py:327
  74.3 1.3 %shard_map.99 = bf16[8,64,768]{2,1,0:T(8,128)(2,1)} custom-call(s32[8,768]{1,0:T(8,128)S(1)} %copy-done.3, bf16[128,768]{1,0:T(8,128)(2,1)S(1)} %get-tuple-element.60.refs_0_, bf16[128,768]{1,0:T(8,128)(2,1)S(1)} %collective-permute-done.13.refs_1_, bf16[8,64,128]{2,1,0:T(8,128)(2,1)S(1)} %get-tuple-element.51.refs_2_, ...), custom_call_target="tpu_custom_call" | custom-call | tf_op jit(solution)/shard_map/pallas_call | solution.py:463
  77.5 2.5 %collective-permute-start.24 = (bf16[8,64,128]{2,1,0:T(8,128)(2,1)S(1)}, bf16[8,64,128]{2,1,0:T(8,128)(2,1)S(1)}, u32[]{:S(2)}, u32[]{:S(2)}) collective-permute-start(bf16[8,64,128]{2,1,0:T(8,128)(2,1)S(1)} %add_convert_fusion.6), channel_id=1, source_target_pairs={{0,8},{4,12},{8,0},{12,4},{1,9},{5,13},{9,1},{13,5},{2,10},{6,14},... | collective-permute-start | bytes 393224 | tf_op jit(solution)/shard_map/ppermute | solution.py:327
  80.1 4.5 %collective-permute-done.24 = bf16[8,64,128]{2,1,0:T(8,128)(2,1)S(1)} collective-permute-done((bf16[8,64,128]{2,1,0:T(8,128)(2,1)S(1)}, bf16[8,64,128]{2,1,0:T(8,128)(2,1)S(1)}, u32[]{:S(2)}, u32[]{:S(2)}) %collective-permute-start.24) | collective-permute-done | bytes 131104 | tf_op jit(solution)/shard_map/ppermute | solution.py:327
  84.7 2.0 %collective-permute-done.20 = bf16[27,16,256]{2,1,0:T(8,128)(2,1)S(1)} collective-permute-done((bf16[27,16,256]{2,1,0:T(8,128)(2,1)S(1)}, bf16[27,16,256]{2,1,0:T(8,128)(2,1)S(1)}, u32[]{:S(2)}, u32[]{:S(2)}) %collective-permute-start.20) | collective-permute-done | bytes 221216 | tf_op jit(solution)/shard_map/ppermute | solution.py:327
  87.0 1.2 %collective-permute-done.21 = bf16[27,16,256]{2,1,0:T(8,128)(2,1)S(1)} collective-permute-done((bf16[27,16,256]{2,1,0:T(8,128)(2,1)S(1)}, bf16[27,16,256]{2,1,0:T(8,128)(2,1)S(1)}, u32[]{:S(2)}, u32[]{:S(2)}) %collective-permute-start.21) | collective-permute-done | bytes 221216 | tf_op jit(solution)/shard_map/ppermute | solution.py:36
  88.3 1.8 %copy-done.7 = f32[27,128,256]{2,1,0:T(8,128)} copy-done((f32[27,128,256]{2,1,0:T(8,128)}, f32[27,128,256]{2,1,0:T(8,128)S(1)}, u32[]{:S(2)}) %copy-start.7) | copy-done | bytes 3538968
  (64 shorter events, 6.1 us)
Async XLA Ops:
  0.6 16.3 %copy-start.6 = (s32[27,768]{1,0:T(8,128)S(1)}, s32[27,768]{1,0:T(8,128)}, u32[]{:S(2)}) copy-start(s32[27,768]{1,0:T(8,128)} %neighbours_ref) | copy-start | bytes 248836
  0.6 17.4 %copy-start.4 = (bf16[128,768]{1,0:T(8,128)(2,1)S(1)}, bf16[128,768]{1,0:T(8,128)(2,1)}, u32[]{:S(2)}) copy-start(bf16[128,768]{1,0:T(8,128)(2,1)} %cotangent_ref.1) | copy-start | bytes 589828
  3.4 8.1 %collective-permute-start = (bf16[768,128]{1,0:T(8,128)(2,1)}, bf16[768,128]{1,0:T(8,128)(2,1)S(1)}, u32[]{:S(2)}, u32[]{:S(2)}) collective-permute-start(bf16[768,128]{1,0:T(8,128)(2,1)} %get-tuple-element.35.refs_0_), channel_id=1, source_target_pairs={{0,2},{2,0},{1,3},{3,1},{4,6},{6,4},{5,7},{7,5},{8,10},{10,8},{9,1... | collective-permute-start | bytes 589832 | tf_op jit(solution)/shard_map/ppermute | solution.py:36
  6.3 11.7 %collective-permute-start.1 = (bf16[768,128]{1,0:T(8,128)(2,1)}, bf16[768,128]{1,0:T(8,128)(2,1)S(1)}, u32[]{:S(2)}, u32[]{:S(2)}) collective-permute-start(bf16[768,128]{1,0:T(8,128)(2,1)} %get-tuple-element.35.refs_0_), channel_id=1, source_target_pairs={{1,4},{5,8},{9,12},{4,1},{8,5},{12,9},{3,6},{7,10},{11,14},{6,3},{... | collective-permute-start | bytes 589832 | tf_op jit(solution)/shard_map/ppermute | solution.py:32
  7.0 11.0 %collective-permute-start.2 = (bf16[768,128]{1,0:T(8,128)(2,1)}, bf16[768,128]{1,0:T(8,128)(2,1)S(1)}, u32[]{:S(2)}, u32[]{:S(2)}) collective-permute-start(bf16[768,128]{1,0:T(8,128)(2,1)} %get-tuple-element.35.refs_0_), channel_id=1, source_target_pairs={{0,1},{1,0},{2,3},{3,2},{4,5},{5,4},{6,7},{7,6},{8,9},{9,8},{10,11... | collective-permute-start | bytes 589832 | tf_op jit(solution)/shard_map/ppermute | solution.py:36
  11.5 6.5 %collective-permute-start.3 = (bf16[768,128]{1,0:T(8,128)(2,1)S(1)}, bf16[768,128]{1,0:T(8,128)(2,1)S(1)}, u32[]{:S(2)}, u32[]{:S(2)}) collective-permute-start(bf16[768,128]{1,0:T(8,128)(2,1)S(1)} %collective-permute-done.refs_3_), channel_id=1, source_target_pairs={{1,4},{5,8},{9,12},{4,1},{8,5},{12,9},{3,6},{7,10},{11,14},{6,3},{... | collective-permute-start | bytes 589832 | tf_op jit(solution)/shard_map/ppermute | solution.py:32
  12.2 5.9 %collective-permute-start.4 = (bf16[768,128]{1,0:T(8,128)(2,1)S(1)}, bf16[768,128]{1,0:T(8,128)(2,1)S(1)}, u32[]{:S(2)}, u32[]{:S(2)}) collective-permute-start(bf16[768,128]{1,0:T(8,128)(2,1)S(1)} %collective-permute-done.refs_3_), channel_id=1, source_target_pairs={{0,1},{1,0},{2,3},{3,2},{4,5},{5,4},{6,7},{7,6},{8,9},{9,8},{10,11... | collective-permute-start | bytes 589832 | tf_op jit(solution)/shard_map/ppermute | solution.py:36
  28.5 25.4 %copy-start.1 = (bf16[8,128,128]{2,1,0:T(8,128)(2,1)S(1)}, bf16[8,128,128]{2,1,0:T(8,128)(2,1)}, u32[]{:S(2)}) copy-start(bf16[8,128,128]{2,1,0:T(8,128)(2,1)} %weight_ref.2) | copy-start | bytes 786436
  28.5 29.8 %copy-start = (bf16[8,128,768]{2,1,0:T(8,128)(2,1)S(1)}, bf16[8,128,768]{2,1,0:T(8,128)(2,1)}, u32[]{:S(2)}) copy-start(bf16[8,128,768]{2,1,0:T(8,128)(2,1)} %children_ref.3) | copy-start | bytes 4718596
  28.5 29.8 %copy-start.2 = (f32[128,768]{1,0:T(8,128)S(1)}, f32[128,768]{1,0:T(8,128)}, u32[]{:S(2)}) copy-start(f32[128,768]{1,0:T(8,128)} %get-tuple-element.55.slope_ref) | copy-start | bytes 1179652
  28.5 29.8 %copy-start.3 = (s32[8,768]{1,0:T(8,128)S(1)}, s32[8,768]{1,0:T(8,128)}, u32[]{:S(2)}) copy-start(s32[8,768]{1,0:T(8,128)} %mask_ref.5) | copy-start | bytes 73732
  28.5 2.1 %collective-permute-start.5 = (bf16[27,16,256]{2,1,0:T(8,128)(2,1)S(1)}, bf16[27,16,256]{2,1,0:T(8,128)(2,1)S(1)}, u32[]{:S(2)}, u32[]{:S(2)}) collective-permute-start(bf16[27,16,256]{2,1,0:T(8,128)(2,1)S(1)} %get-tuple-element.43), channel_id=1, source_target_pairs={{0,1},{1,0},{2,3},{3,2},{4,5},{5,4},{6,7},{7,6},{8,9},{9,8},{10,11... | collective-permute-start | bytes 663560 | tf_op jit(solution)/shard_map/ppermute | solution.py:36
  30.7 2.2 %collective-permute-start.6 = (bf16[3,27,16,256]{3,2,1,0:T(8,128)(2,1)S(1)}, bf16[3,27,16,256]{3,2,1,0:T(8,128)(2,1)S(1)}, u32[]{:S(2)}, u32[]{:S(2)}) collective-permute-start(bf16[3,27,16,256]{3,2,1,0:T(8,128)(2,1)S(1)} %get-tuple-element.44), channel_id=1, source_target_pairs={{0,1},{1,0},{2,3},{3,2},{4,5},{5,4},{6,7},{7,6},{8,9},{9,8},{10,11... | collective-permute-start | bytes 1990664 | tf_op jit(solution)/shard_map/ppermute | solution.py:36
  31.2 8.0 %collective-permute-start.9 = (bf16[27,16,256]{2,1,0:T(8,128)(2,1)S(1)}, bf16[27,16,256]{2,1,0:T(8,128)(2,1)S(1)}, u32[]{:S(2)}, u32[]{:S(2)}) collective-permute-start(bf16[27,16,256]{2,1,0:T(8,128)(2,1)S(1)} %fusion), channel_id=1, source_target_pairs={{0,4},{4,0},{8,12},{12,8},{1,5},{5,1},{9,13},{13,9},{2,6},{6,2},{1... | collective-permute-start | bytes 663560 | tf_op jit(solution)/shard_map/ppermute | solution.py:327
  33.8 4.2 %collective-permute-start.7 = (bf16[768,128]{1,0:T(8,128)(2,1)S(1)}, bf16[768,128]{1,0:T(8,128)(2,1)S(1)}, u32[]{:S(2)}, u32[]{:S(2)}) collective-permute-start(bf16[768,128]{1,0:T(8,128)(2,1)S(1)} %get-tuple-element.46.refs_0_), channel_id=1, source_target_pairs={{1,4},{5,8},{9,12},{4,1},{8,5},{12,9},{3,6},{7,10},{11,14},{6,3},{... | collective-permute-start | bytes 589832 | tf_op jit(solution)/shard_map/ppermute | solution.py:32
  34.7 4.4 %collective-permute-start.8 = (bf16[768,128]{1,0:T(8,128)(2,1)S(1)}, bf16[768,128]{1,0:T(8,128)(2,1)S(1)}, u32[]{:S(2)}, u32[]{:S(2)}) collective-permute-start(bf16[768,128]{1,0:T(8,128)(2,1)S(1)} %get-tuple-element.46.refs_0_), channel_id=1, source_target_pairs={{0,1},{1,0},{2,3},{3,2},{4,5},{5,4},{6,7},{7,6},{8,9},{9,8},{10,11... | collective-permute-start | bytes 589832 | tf_op jit(solution)/shard_map/ppermute | solution.py:36
  39.9 19.8 %collective-permute-start.12 = (bf16[27,16,256]{2,1,0:T(8,128)(2,1)}, bf16[27,16,256]{2,1,0:T(8,128)(2,1)S(1)}, u32[]{:S(2)}, u32[]{:S(2)}) collective-permute-start(bf16[27,16,256]{2,1,0:T(8,128)(2,1)} %get-tuple-element.59), channel_id=1, source_target_pairs={{0,4},{4,0},{8,12},{12,8},{1,5},{5,1},{9,13},{13,9},{2,6},{6,2},{1... | collective-permute-start | bytes 663560 | tf_op jit(solution)/shard_map/ppermute | solution.py:327
  43.5 16.2 %collective-permute-start.11 = (bf16[27,16,256]{2,1,0:T(8,128)(2,1)}, bf16[27,16,256]{2,1,0:T(8,128)(2,1)}, u32[]{:S(2)}, u32[]{:S(2)}) collective-permute-start(bf16[27,16,256]{2,1,0:T(8,128)(2,1)} %add_convert_fusion.3), channel_id=1, source_target_pairs={{0,8},{4,12},{8,0},{12,4},{1,9},{5,13},{9,1},{13,5},{2,10},{6,14},... | collective-permute-start | bytes 663560 | tf_op jit(solution)/shard_map/ppermute | solution.py:327
  52.5 5.9 %collective-permute-start.10 = (bf16[128,768]{1,0:T(8,128)(2,1)S(1)}, bf16[128,768]{1,0:T(8,128)(2,1)S(1)}, u32[]{:S(2)}, u32[]{:S(2)}) collective-permute-start(bf16[128,768]{1,0:T(8,128)(2,1)S(1)} %bitcast.10), channel_id=1, source_target_pairs={{0,2},{2,0},{1,3},{3,1},{4,6},{6,4},{5,7},{7,5},{8,10},{10,8},{9,1... | collective-permute-start | bytes 589832 | tf_op jit(solution)/shard_map/ppermute | solution.py:418
  59.6 4.6 %collective-permute-start.22 = (bf16[8,64,128]{2,1,0:T(8,128)(2,1)S(1)}, bf16[8,64,128]{2,1,0:T(8,128)(2,1)S(1)}, u32[]{:S(2)}, u32[]{:S(2)}) collective-permute-start(bf16[8,64,128]{2,1,0:T(8,128)(2,1)S(1)} %get-tuple-element.64), channel_id=1, source_target_pairs={{0,1},{1,0},{2,3},{3,2},{4,5},{5,4},{6,7},{7,6},{8,9},{9,8},{10,11... | collective-permute-start | bytes 393224 | tf_op jit(solution)/shard_map/ppermute | solution.py:36
  60.7 15.3 %collective-permute-start.18 = (bf16[27,16,256]{2,1,0:T(8,128)(2,1)S(1)}, bf16[27,16,256]{2,1,0:T(8,128)(2,1)S(1)}, u32[]{:S(2)}, u32[]{:S(2)}) collective-permute-start(bf16[27,16,256]{2,1,0:T(8,128)(2,1)S(1)} %add_convert_fusion), channel_id=1, source_target_pairs={{0,8},{4,12},{8,0},{12,4},{1,9},{5,13},{9,1},{13,5},{2,10},{6,14},... | collective-permute-start | bytes 663560 | tf_op jit(solution)/shard_map/ppermute | solution.py:327
  62.4 14.2 %collective-permute-start.15 = (bf16[27,16,256]{2,1,0:T(8,128)(2,1)S(1)}, bf16[27,16,256]{2,1,0:T(8,128)(2,1)S(1)}, u32[]{:S(2)}, u32[]{:S(2)}) collective-permute-start(bf16[27,16,256]{2,1,0:T(8,128)(2,1)S(1)} %add_convert_fusion), channel_id=1, source_target_pairs={{0,1},{1,0},{2,3},{3,2},{4,5},{5,4},{6,7},{7,6},{8,9},{9,8},{10,11... | collective-permute-start | bytes 663560 | tf_op jit(solution)/shard_map/ppermute | solution.py:36
  62.6 13.9 %collective-permute-start.16 = (bf16[27,16,256]{2,1,0:T(8,128)(2,1)S(1)}, bf16[27,16,256]{2,1,0:T(8,128)(2,1)S(1)}, u32[]{:S(2)}, u32[]{:S(2)}) collective-permute-start(bf16[27,16,256]{2,1,0:T(8,128)(2,1)S(1)} %add_convert_fusion), channel_id=1, source_target_pairs={{0,4},{4,0},{8,12},{12,8},{1,5},{5,1},{9,13},{13,9},{2,6},{6,2},{1... | collective-permute-start | bytes 663560 | tf_op jit(solution)/shard_map/ppermute | solution.py:327
  62.7 11.6 %collective-permute-start.14 = (bf16[8,64,128]{2,1,0:T(8,128)(2,1)S(1)}, bf16[8,64,128]{2,1,0:T(8,128)(2,1)S(1)}, u32[]{:S(2)}, u32[]{:S(2)}) collective-permute-start(bf16[8,64,128]{2,1,0:T(8,128)(2,1)S(1)} %get-tuple-element.61), channel_id=1, source_target_pairs={{0,2},{2,0},{1,3},{3,1},{4,6},{6,4},{5,7},{7,5},{8,10},{10,8},{9,1... | collective-permute-start | bytes 393224 | tf_op jit(solution)/shard_map/ppermute | solution.py:458
  64.2 8.3 %collective-permute-start.13 = (bf16[128,768]{1,0:T(8,128)(2,1)S(1)}, bf16[128,768]{1,0:T(8,128)(2,1)S(1)}, u32[]{:S(2)}, u32[]{:S(2)}) collective-permute-start(bf16[128,768]{1,0:T(8,128)(2,1)S(1)} %get-tuple-element.60.refs_0_), channel_id=1, source_target_pairs={{0,2},{2,0},{1,3},{3,1},{4,6},{6,4},{5,7},{7,5},{8,10},{10,8},{9,1... | collective-permute-start | bytes 589832 | tf_op jit(solution)/shard_map/ppermute | solution.py:452
  72.5 5.0 %collective-permute-start.23 = (bf16[8,64,128]{2,1,0:T(8,128)(2,1)S(1)}, bf16[8,64,128]{2,1,0:T(8,128)(2,1)S(1)}, u32[]{:S(2)}, u32[]{:S(2)}) collective-permute-start(bf16[8,64,128]{2,1,0:T(8,128)(2,1)S(1)} %add_convert_fusion.7), channel_id=1, source_target_pairs={{0,4},{4,0},{8,12},{12,8},{1,5},{5,1},{9,13},{13,9},{2,6},{6,2},{1... | collective-permute-start | bytes 393224 | tf_op jit(solution)/shard_map/ppermute | solution.py:327
  76.0 10.8 %collective-permute-start.19 = (bf16[27,16,256]{2,1,0:T(8,128)(2,1)S(1)}, bf16[27,16,256]{2,1,0:T(8,128)(2,1)S(1)}, u32[]{:S(2)}, u32[]{:S(2)}) collective-permute-start(bf16[27,16,256]{2,1,0:T(8,128)(2,1)S(1)} %collective-permute-done.18), channel_id=1, source_target_pairs={{0,1},{1,0},{2,3},{3,2},{4,5},{5,4},{6,7},{7,6},{8,9},{9,8},{10,11... | collective-permute-start | bytes 663560 | tf_op jit(solution)/shard_map/ppermute | solution.py:36
  76.1 10.7 %collective-permute-start.20 = (bf16[27,16,256]{2,1,0:T(8,128)(2,1)S(1)}, bf16[27,16,256]{2,1,0:T(8,128)(2,1)S(1)}, u32[]{:S(2)}, u32[]{:S(2)}) collective-permute-start(bf16[27,16,256]{2,1,0:T(8,128)(2,1)S(1)} %collective-permute-done.18), channel_id=1, source_target_pairs={{0,4},{4,0},{8,12},{12,8},{1,5},{5,1},{9,13},{13,9},{2,6},{6,2},{1... | collective-permute-start | bytes 663560 | tf_op jit(solution)/shard_map/ppermute | solution.py:327
  76.5 10.3 %collective-permute-start.17 = (bf16[27,16,256]{2,1,0:T(8,128)(2,1)S(1)}, bf16[27,16,256]{2,1,0:T(8,128)(2,1)S(1)}, u32[]{:S(2)}, u32[]{:S(2)}) collective-permute-start(bf16[27,16,256]{2,1,0:T(8,128)(2,1)S(1)} %collective-permute-done.16), channel_id=1, source_target_pairs={{0,1},{1,0},{2,3},{3,2},{4,5},{5,4},{6,7},{7,6},{8,9},{9,8},{10,11... | collective-permute-start | bytes 663560 | tf_op jit(solution)/shard_map/ppermute | solution.py:36
  77.5 7.0 %collective-permute-start.24 = (bf16[8,64,128]{2,1,0:T(8,128)(2,1)S(1)}, bf16[8,64,128]{2,1,0:T(8,128)(2,1)S(1)}, u32[]{:S(2)}, u32[]{:S(2)}) collective-permute-start(bf16[8,64,128]{2,1,0:T(8,128)(2,1)S(1)} %add_convert_fusion.6), channel_id=1, source_target_pairs={{0,8},{4,12},{8,0},{12,4},{1,9},{5,13},{9,1},{13,5},{2,10},{6,14},... | collective-permute-start | bytes 393224 | tf_op jit(solution)/shard_map/ppermute | solution.py:327
  84.7 2.3 %collective-permute-start.25 = (bf16[8,64,128]{2,1,0:T(8,128)(2,1)S(1)}, bf16[8,64,128]{2,1,0:T(8,128)(2,1)S(1)}, u32[]{:S(2)}, u32[]{:S(2)}) collective-permute-start(bf16[8,64,128]{2,1,0:T(8,128)(2,1)S(1)} %get-tuple-element.67), channel_id=1, source_target_pairs={{0,1},{1,0},{2,3},{3,2},{4,5},{5,4},{6,7},{7,6},{8,9},{9,8},{10,11... | collective-permute-start | bytes 393224 | tf_op jit(solution)/shard_map/ppermute | solution.py:36
  86.8 1.5 %collective-permute-start.21 = (bf16[27,16,256]{2,1,0:T(8,128)(2,1)S(1)}, bf16[27,16,256]{2,1,0:T(8,128)(2,1)S(1)}, u32[]{:S(2)}, u32[]{:S(2)}) collective-permute-start(bf16[27,16,256]{2,1,0:T(8,128)(2,1)S(1)} %collective-permute-done.20), channel_id=1, source_target_pairs={{0,1},{1,0},{2,3},{3,2},{4,5},{5,4},{6,7},{7,6},{8,9},{9,8},{10,11... | collective-permute-start | bytes 663560 | tf_op jit(solution)/shard_map/ppermute | solution.py:36
  (3 other events, 17.7 us)
